TPU v7x, 32 devices: a whole 2x2x4 slice. The times are simulated.
32 devices in a mesh: cuts: 2 (over core), fsdp: 4 (over y, x), tp: 4 (over z).
Axes of the slice: x: 2, y: 2, z: 4, core: 2. Of those that a mesh axis runs over, the one named last changes fastest.
Arguments:
- tokens: bfloat16 [8192, 2048], P(('cuts', 'fsdp')), may hold values from -6 to 6
- cotangent: bfloat16 [8192, 2048], P(('cuts', 'fsdp')), may hold values from -6 to 6
- gate_frozen_matrix: bfloat16 [2048, 4096], P(('cuts', 'fsdp'), 'tp'), may hold values from -0.125 to 0.125
- up_frozen_matrix: bfloat16 [2048, 4096], P(('cuts', 'fsdp'), 'tp'), may hold values from -0.125 to 0.125
- down_frozen_matrix: bfloat16 [4096, 2048], P('tp', ('cuts', 'fsdp')), may hold values from -0.09375 to 0.09375
- gate_adapter_input_factor: bfloat16 [2048, 64], replicated, may hold values from -0.125 to 0.125
- up_adapter_input_factor: bfloat16 [2048, 64], replicated, may hold values from -0.125 to 0.125
- gate_adapter_output_factor: bfloat16 [64, 4096], P(None, 'tp'), may hold values from -0.75 to 0.75
- up_adapter_output_factor: bfloat16 [64, 4096], P(None, 'tp'), may hold values from -0.75 to 0.75
- down_adapter_input_factor: bfloat16 [4096, 64], P('tp'), may hold values from -0.09375 to 0.09375
- down_leave: bfloat16 [2048, 64], replicated, may hold values from -0.75 to 0.75
Outputs:
- token_input_gradient: bfloat16 [8192, 2048], P(('cuts', 'fsdp'), 'tp')
- wide_grads: float32 [2048, 192], P(('cuts', 'fsdp', 'tp'))
- narrow_grads: float32 [4096, 192], P('tp')
All inputs are finite; a program needn't handle non-finite values.
Results may differ from a plain program's by a relative error of at most 0.0055.
Values may be sent and summed in bfloat16 or wider, within the bound.
No kernel may reach another device: no remote copies, remote signals or barrier semaphores. Data moves between devices by JAX's collectives and lax.ppermute only.
A program may use at most 128 MiB of HBM per device.

v0:
```python
import math

import jax
import jax.numpy as jnp
from jax import lax
from jax.sharding import PartitionSpec as P

adapter_scaling = 0.5


def matrix_product(left, right):
    return jnp.dot(left, right, preferred_element_type=jnp.float32)


def contract_trailing_axis(left, right):
    return lax.dot_general(
        left, right, (((1,), (1,)), ((), ())), preferred_element_type=jnp.float32
    )


def contract_first(left, right):
    return lax.dot_general(
        left, right, (((0,), (0,)), ((), ())), preferred_element_type=jnp.float32
    )


def per_device(
    tokens,
    cotangent,
    gate_frozen_matrix,
    up_frozen_matrix,
    down_frozen_matrix,
    gate_adapter_input_factor,
    up_adapter_input_factor,
    gate_adapter_output_factor,
    up_adapter_output_factor,
    down_adapter_input_factor,
    down_leave,
):
    token_groups = lax.axis_size(("cuts", "fsdp"))
    quarters = lax.axis_size("tp")
    tp_index = lax.axis_index("tp")
    token_rows = tokens.shape[0]
    width = tokens.shape[1]
    gradient_scaling = adapter_scaling / math.sqrt(token_rows * token_groups)
    gate_adapter_hidden = matrix_product(tokens, gate_adapter_input_factor).astype(jnp.bfloat16)
    up_adapter_hidden = matrix_product(tokens, up_adapter_input_factor).astype(jnp.bfloat16)
    pieces = (
        lax.all_gather(gate_frozen_matrix, ("cuts", "fsdp"), axis=0, tiled=True),
        lax.all_gather(up_frozen_matrix, ("cuts", "fsdp"), axis=0, tiled=True),
    )
    columns = tokens
    gate_frozen_output = matrix_product(columns, pieces[0])
    up_frozen_output = matrix_product(columns, pieces[1])
    gate_preactivation = gate_frozen_output + adapter_scaling * matrix_product(
        gate_adapter_hidden, gate_adapter_output_factor
    )
    up_preactivation = up_frozen_output + adapter_scaling * matrix_product(
        up_adapter_hidden, up_adapter_output_factor
    )
    sig = jax.nn.sigmoid(gate_preactivation)
    hidden = (gate_preactivation * sig * up_preactivation).astype(jnp.bfloat16)
    down_part = matrix_product(hidden, down_adapter_input_factor)
    down_low = lax.psum(down_part.astype(jnp.bfloat16), "tp")
    backward_adapter_input = matrix_product(cotangent, down_leave).astype(jnp.bfloat16)
    columns = cotangent
    hidden_state_gradient = contract_trailing_axis(
        columns, lax.all_gather(down_frozen_matrix, ("cuts", "fsdp"), axis=1, tiled=True)
    )
    hidden_state_gradient = hidden_state_gradient + adapter_scaling * contract_trailing_axis(
        backward_adapter_input, down_adapter_input_factor
    )
    gate_output_gradient = (
        hidden_state_gradient * up_preactivation * sig * (1.0 + gate_preactivation * (1.0 - sig))
    ).astype(jnp.bfloat16)
    up_output_gradient = (hidden_state_gradient * gate_preactivation * sig).astype(jnp.bfloat16)
    gate_part = contract_trailing_axis(gate_output_gradient, gate_adapter_output_factor)
    up_part = contract_trailing_axis(up_output_gradient, up_adapter_output_factor)
    gate_sum, up_sum = lax.psum((gate_part, up_part), "tp")
    gate_backward_adapter = gate_sum.astype(jnp.bfloat16)
    up_backward_adapter = up_sum.astype(jnp.bfloat16)
    pieces = lax.all_gather(
        (gate_frozen_matrix, up_frozen_matrix), ("cuts", "fsdp"), axis=0, tiled=True
    )
    partial_value = contract_trailing_axis(
        gate_output_gradient, pieces[0]
    ) + contract_trailing_axis(up_output_gradient, pieces[1])
    frozen_path_gradient = lax.psum_scatter(partial_value, "tp", scatter_dimension=1, tiled=True)
    slice_width = width // quarters
    gate_slice = lax.dynamic_slice_in_dim(
        gate_adapter_input_factor, tp_index * slice_width, slice_width, 0
    )
    up_slice = lax.dynamic_slice_in_dim(
        up_adapter_input_factor, tp_index * slice_width, slice_width, 0
    )
    adapter_hidden_gradient = contract_trailing_axis(
        gate_backward_adapter, gate_slice
    ) + contract_trailing_axis(up_backward_adapter, up_slice)
    token_input_gradient = (
        frozen_path_gradient + adapter_scaling * adapter_hidden_gradient
    ).astype(jnp.bfloat16)
    narrow_part = gradient_scaling * jnp.concatenate(
        [
            contract_first(hidden, backward_adapter_input),
            contract_first(gate_output_gradient, gate_adapter_hidden),
            contract_first(up_output_gradient, up_adapter_hidden),
        ],
        axis=1,
    )
    narrow_grads = lax.psum(narrow_part, ("cuts", "fsdp"))
    token_side = jnp.concatenate([gate_backward_adapter, up_backward_adapter], axis=1)
    group_rows = lax.psum_scatter(
        gradient_scaling
        * jnp.concatenate(
            [contract_first(tokens, token_side), contract_first(cotangent, down_low)], axis=1
        ),
        ("cuts", "fsdp"),
        scatter_dimension=0,
        tiled=True,
    )
    fine_rows = width // (token_groups * quarters)
    wide_grads = lax.dynamic_slice_in_dim(group_rows, tp_index * fine_rows, fine_rows, 0)
    return (token_input_gradient, wide_grads, narrow_grads)


def solution(mesh):
    in_specs = (
        P(("cuts", "fsdp"), None),
        P(("cuts", "fsdp"), None),
        P(("cuts", "fsdp"), "tp"),
        P(("cuts", "fsdp"), "tp"),
        P("tp", ("cuts", "fsdp")),
        P(),
        P(),
        P(None, "tp"),
        P(None, "tp"),
        P("tp", None),
        P(),
    )
    out_specs = (P(("cuts", "fsdp"), "tp"), P(("cuts", "fsdp", "tp"), None), P("tp", None))
    return jax.shard_map(
        per_device, mesh=mesh, in_specs=in_specs, out_specs=out_specs, check_vma=False
    )
```

profile of v0, /device:TPU:0, one launch (start us, length us, event | category | flops | bytes accessed | tf_op | source)
XLA Modules:
  0.0 438.3 jit_solution(11265776863674347428)
XLA Ops:
  7.2 0.0 copy-start
  7.2 0.0 copy-start.16
  7.2 0.0 all-gather.8.cloned.1.call-start
  7.2 0.7 all-gather.8.cloned.1.call-update
  7.9 0.0 all-gather.4.cloned.1.call-start
  8.0 0.7 all-gather.4.cloned.1.call-update
  8.7 0.0 all-gather.6.cloned.1.call-start
  8.7 0.7 all-gather.6.cloned.1.call-update
  9.4 0.0 all-reduce.5.cloned.1.call-start
  9.5 0.0 copy-done
  9.5 0.0 copy-start.1
  9.5 3.7 convolution_convert_fusion.1
  13.2 0.0 copy-done.16
  13.2 0.0 copy-done.1
  13.2 0.0 copy-start.8
  13.2 0.0 copy-start.2
  13.2 0.0 copy-start.17
  13.3 1.4 convolution_convert_fusion.2
  14.7 0.8 copy-done.2
  15.5 0.0 copy-done.17
  15.5 1.4 convolution_convert_fusion.3
  16.9 32.5 %all-gather.8.cloned.1.call-done = bf16[2048,1024]{1,0:T(8,128)(2,1)} async-done(((bf16[256,1024]{1,0:T(8,128)(2,1)}), bf16[2048,1024]{1,0:T(8,128)(2,1)}) %all-gather.8.cloned.1.call-update) | async-done | bytes 4194320 | tf_op jit(solution)/shard_map/all_gather | solution.py:49
  49.4 7.5 %fusion.11 = f32[1024,1024]{1,0:T(8,128)S(1)} fusion(bf16[1024,2048]{1,0:T(8,128)(2,1)} %param.11, bf16[2048,1024]{1,0:T(8,128)(2,1)} %all-gather.8.cloned.1.call-done), kind=kOutput, calls=%fused_computation.29 | convolution fusion | flops 4294967296 | bytes 12582912 | tf_op jit(solution)/shard_map/dot_general | solution.py:12
  56.9 0.0 copy-done.8
  56.9 0.0 copy-done.12
  56.9 2.7 multiply_add_fusion
  59.6 29.1 %all-gather.4.cloned.1.call-done = bf16[1024,2048]{1,0:T(8,128)(2,1)} async-done(((bf16[1024,256]{1,0:T(8,128)(2,1)}), bf16[1024,2048]{1,0:T(8,128)(2,1)}) %all-gather.4.cloned.1.call-update) | async-done | bytes 4194320 | tf_op jit(solution)/shard_map/all_gather | solution.py:68
  88.7 7.6 %fusion.9 = f32[1024,1024]{1,0:T(8,128)S(1)} fusion(bf16[1024,2048]{1,0:T(8,128)(2,1)} %param.12, bf16[1024,2048]{1,0:T(8,128)(2,1)} %all-gather.4.cloned.1.call-done), kind=kOutput, calls=%fused_computation.27 | convolution fusion | flops 4294967296 | bytes 12582912 | tf_op jit(solution)/shard_map/dot_general | solution.py:16
  96.3 2.7 multiply_add_fusion.2
  99.0 28.3 %all-gather.6.cloned.1.call-done = bf16[2048,1024]{1,0:T(8,128)(2,1)} async-done(((bf16[256,1024]{1,0:T(8,128)(2,1)}), bf16[2048,1024]{1,0:T(8,128)(2,1)}) %all-gather.6.cloned.1.call-update) | async-done | bytes 4194320 | tf_op jit(solution)/shard_map/all_gather | solution.py:50
  127.3 7.6 %fusion.10 = f32[1024,1024]{1,0:T(8,128)S(1)} fusion(bf16[1024,2048]{1,0:T(8,128)(2,1)} %param.11, bf16[2048,1024]{1,0:T(8,128)(2,1)} %all-gather.6.cloned.1.call-done), kind=kOutput, calls=%fused_computation.28 | convolution fusion | flops 4294967296 | bytes 12582912 | tf_op jit(solution)/shard_map/dot_general | solution.py:12
  135.0 0.0 copy-done.10
  135.0 2.8 multiply_convert_fusion
  137.9 0.8 fusion.13
  138.7 0.6 copy-done.3
  139.3 0.8 fusion.14
  140.0 1.4 convolution_convert_fusion
  141.4 0.0 all-reduce.5.cloned.1.call-update
  141.4 0.0 reduce-scatter.5.cloned.1.call-start
  141.5 33.8 %all-reduce.8 = (bf16[1024,64]{0,1:T(8,128)(2,1)}, bf16[1024,64]{0,1:T(8,128)(2,1)}) all-reduce(f32[1024,64]{0,1:T(8,128)S(1)} %fusion.13, f32[1024,64]{0,1:T(8,128)S(1)} %fusion.14), channel_id=1, replica_groups=mesh['cuts'=2,'fsdp'=4,'tp'=4] {'tp'}, use_global_device_ids=true, to_apply=%region_1.0 | all-reduce | flops 131072 | bytes 786432 | tf_op jit(solution)/shard_map/psum | solution.py:79
  175.3 3.1 convolution_bitcast_fusion
  178.4 1.2 all-reduce.5.cloned.1.call-done
  179.6 3.1 convolution_bitcast_fusion.1
  182.7 1.3 maximum_multiply_fusion
  184.0 0.0 reduce-scatter.5.cloned.1.call-update
  184.1 0.0 reduce-scatter.3.cloned.1.call-start
  184.1 7.4 %fusion.12 = f32[1024,2048]{1,0:T(8,128)S(1)} fusion(bf16[1024,1024]{1,0:T(8,128)(2,1)} %copy-done.5, bf16[2048,1024]{1,0:T(8,128)(2,1)} %all-gather.8.cloned.1.call-done), kind=kOutput, calls=%fused_computation.30 | convolution fusion | flops 4294967296 | bytes 14680064 | tf_op jit(solution)/shard_map/dot_general | solution.py:16
  191.5 6.9 %convolution_add_fusion = f32[1024,2048]{1,0:T(8,128)} fusion(f32[1024,2048]{1,0:T(8,128)S(1)} %fusion.12, bf16[1024,1024]{1,0:T(8,128)(2,1)S(1)} %copy-done.4, bf16[2048,1024]{1,0:T(8,128)(2,1)S(1)} %copy-done.19), kind=kOutput, calls=%fused_computation.7 | convolution fusion | flops 4297064448 | bytes 23068672 | tf_op jit(solution)/shard_map/dot_general | solution.py:16
  198.5 0.0 reduce-scatter.3.cloned.1.call-update
  198.5 0.0 all-reduce.7.cloned.1.call-start
  198.5 0.8 copy-done.9
  199.4 2.1 fusion.16
  201.5 2.1 fusion.17
  203.6 0.5 fusion.15
  204.0 1.0 maximum_multiply_fusion.1
  205.0 0.5 fusion.4
  205.5 0.0 all-reduce.7.cloned.1.call-update
  205.5 16.8 %reduce-scatter.5.cloned.1.call-done = f32[256,192]{0,1:T(8,128)} async-done(((f32[2048,192]{0,1:T(8,128)}), f32[256,192]{0,1:T(8,128)}) %reduce-scatter.5.cloned.1.call-update) | async-done | bytes 196624 | tf_op jit(solution)/shard_map/reduce_scatter | solution.py:112
  222.3 1.0 constant_dynamic-slice_fusion
  223.2 0.7 copy.14
  224.0 145.1 %reduce-scatter.3.cloned.1.call-done = f32[1024,512]{1,0:T(8,128)} async-done(((f32[1024,2048]{1,0:T(8,128)}), f32[1024,512]{1,0:T(8,128)}) %reduce-scatter.3.cloned.1.call-update) | async-done | bytes 2097168 | tf_op jit(solution)/shard_map/reduce_scatter | solution.py:88
  369.1 3.1 add_convert_fusion
  372.1 57.3 %all-reduce.7.cloned.1.call-done = f32[1024,192]{0,1:T(8,128)} async-done(((f32[1024,192]{0,1:T(8,128)}), f32[1024,192]{0,1:T(8,128)}) %all-reduce.7.cloned.1.call-update) | async-done | bytes 786448 | tf_op jit(solution)/shard_map/psum | solution.py:110
  429.4 2.1 copy.21
  (24 shorter events, 0.0 us)
Async XLA Ops:
  7.2 2.3 copy-start
  7.2 6.0 %copy-start.16 = (bf16[2048,64]{0,1:T(8,128)(2,1)S(1)}, bf16[2048,64]{0,1:T(8,128)(2,1)}, u32[]{:S(2)}) copy-start(bf16[2048,64]{0,1:T(8,128)(2,1)} %param.17) | copy-start | bytes 786436
  7.2 42.2 %all-gather.8.cloned.1.call-start = ((), (), s32[]{:S(2)}) async-start(), calls=%async_computation.4 | async-start | bytes 4718592 | tf_op jit(solution)/shard_map/all_gather | solution.py:49
  7.9 80.8 %all-gather.4.cloned.1.call-start = ((), (), s32[]{:S(2)}) async-start(), calls=%async_computation.2 | async-start | bytes 4718592 | tf_op jit(solution)/shard_map/all_gather | solution.py:68
  8.7 118.7 %all-gather.6.cloned.1.call-start = ((), (), s32[]{:S(2)}) async-start(), calls=%async_computation.3 | async-start | bytes 4718592 | tf_op jit(solution)/shard_map/all_gather | solution.py:50
  9.4 170.1 %all-reduce.5.cloned.1.call-start = ((), (), s32[]{:S(2)}) async-start(), calls=%async_computation.6 | async-start | bytes 524288 | tf_op jit(solution)/shard_map/psum | solution.py:64
  9.5 3.8 copy-start.1
  13.2 43.6 %copy-start.8 = (bf16[1024,64]{0,1:T(8,128)(2,1)}, bf16[1024,64]{0,1:T(8,128)(2,1)S(1)}, u32[]{:S(2)}) copy-start(bf16[1024,64]{0,1:T(8,128)(2,1)S(1)} %convolution_convert_fusion.1) | copy-start | bytes 393220
  13.2 2.2 copy-start.2
  13.2 2.2 copy-start.17
  15.5 119.5 %copy-start.10 = (bf16[1024,64]{0,1:T(8,128)(2,1)}, bf16[1024,64]{0,1:T(8,128)(2,1)S(1)}, u32[]{:S(2)}) copy-start(bf16[1024,64]{0,1:T(8,128)(2,1)S(1)} %convolution_convert_fusion.2) | copy-start | bytes 393220
  16.9 40.0 %copy-start.12 = (bf16[64,1024]{1,0:T(8,128)(2,1)S(1)}, bf16[64,1024]{1,0:T(8,128)(2,1)}, u32[]{:S(2)}) copy-start(bf16[64,1024]{1,0:T(8,128)(2,1)} %param.18) | copy-start | bytes 393220
  59.6 36.7 %copy-start.13 = (bf16[1024,64]{0,1:T(8,128)(2,1)S(1)}, bf16[1024,64]{0,1:T(8,128)(2,1)}, u32[]{:S(2)}) copy-start(bf16[1024,64]{0,1:T(8,128)(2,1)} %param.20) | copy-start | bytes 393220
  99.0 36.0 %copy-start.18 = (bf16[64,1024]{1,0:T(8,128)(2,1)S(1)}, bf16[64,1024]{1,0:T(8,128)(2,1)}, u32[]{:S(2)}) copy-start(bf16[64,1024]{1,0:T(8,128)(2,1)} %param.19) | copy-start | bytes 393220
  127.3 7.7 %copy-start.6 = (f32[1024,1024]{1,0:T(8,128)S(1)}, f32[1024,1024]{1,0:T(8,128)}, u32[]{:S(2)}) copy-start(f32[1024,1024]{1,0:T(8,128)} %multiply_add_fusion) | copy-start | bytes 12582916
  127.3 7.7 %copy-start.7 = (f32[1024,1024]{1,0:T(8,128)S(1)}, f32[1024,1024]{1,0:T(8,128)}, u32[]{:S(2)}) copy-start(f32[1024,1024]{1,0:T(8,128)} %multiply_add_fusion.2) | copy-start | bytes 12582916
  137.9 1.4 copy-start.3
  137.9 2.1 copy-start.5
  141.4 80.8 %reduce-scatter.5.cloned.1.call-start = ((), (), s32[]{:S(2)}) async-start(), calls=%async_computation.7 | async-start | bytes 1769472 | tf_op jit(solution)/shard_map/reduce_scatter | solution.py:112
  184.1 185.0 %reduce-scatter.3.cloned.1.call-start = ((), (), s32[]{:S(2)}) async-start(), calls=%async_computation.5 | async-start | bytes 10485760 | tf_op jit(solution)/shard_map/reduce_scatter | solution.py:88
  184.1 7.4 %copy-start.4 = (bf16[1024,1024]{1,0:T(8,128)(2,1)S(1)}, bf16[1024,1024]{1,0:T(8,128)(2,1)}, u32[]{:S(2)}) copy-start(bf16[1024,1024]{1,0:T(8,128)(2,1)} %copy-done.3) | copy-start | bytes 6291460
  184.1 7.4 %copy-start.19 = (bf16[2048,1024]{1,0:T(8,128)(2,1)S(1)}, bf16[2048,1024]{1,0:T(8,128)(2,1)}, u32[]{:S(2)}) copy-start(bf16[2048,1024]{1,0:T(8,128)(2,1)} %all-gather.6.cloned.1.call-done) | copy-start | bytes 12582916
  198.4 0.9 copy-start.9
  198.5 3.0 copy-start.11
  198.5 230.9 %all-reduce.7.cloned.1.call-start = ((), (), s32[]{:S(2)}) async-start(), calls=%async_computation.8 | async-start | bytes 1572864 | tf_op jit(solution)/shard_map/psum | solution.py:110
  199.4 5.6 %copy-start.15 = (bf16[1024,64]{0,1:T(8,128)(2,1)S(1)}, bf16[1024,64]{0,1:T(8,128)(2,1)}, u32[]{:S(2)}) copy-start(bf16[1024,64]{0,1:T(8,128)(2,1)} %get-tuple-element.6) | copy-start | bytes 393220
  203.5 165.5 %copy-start.14 = (bf16[1024,64]{0,1:T(8,128)(2,1)S(1)}, bf16[1024,64]{0,1:T(8,128)(2,1)}, u32[]{:S(2)}) copy-start(bf16[1024,64]{0,1:T(8,128)(2,1)} %get-tuple-element.7) | copy-start | bytes 393220
Sparse Core Ops, SparseCore 0:
  9.9 39.4 all-gather.7
  51.2 37.4 all-gather.3
  90.6 36.7 all-gather.5
  141.6 37.9 all-reduce.4
  184.2 38.0 reduce-scatter.4
  224.6 144.4 reduce-scatter.2
  373.1 56.2 all-reduce.6
where the time goes:
time: 439 us; the launch traced here: 438 us
  waiting for transfers between devices  312 us (71%)
  matrix products  69 us (16%)
  blocking collectives  33.8 us (8%)
  between operations  14.4 us (3%)
  local copies, waits for them, and re-layouts  6.14 us (1%)
    reduce_scatter x1, waiting for transfers between devices, per_device(): lax.psum_scatter(partial_value, 'tp', scatter_dimension=1, tiled=True)  145 us
    psum x1, waiting for transfers between devices, per_device(): narrow_grads = lax.psum(narrow_part, ('cuts', 'fsdp'))  57.3 us
    psum x1, blocking collectives, per_device(): gate_sum, up_sum = lax.psum((gate_part, up_part), 'tp')  33.8 us
    all_gather x1, waiting for transfers between devices, per_device(): lax.all_gather(gate_frozen_matrix, ('cuts', 'fsdp'), axis=0, tiled=True)  32.5 us
    dot_general x8, matrix products, contract_trailing_axis(): lax.dot_general(left, right, (((1,), (1,)), ((), ())), preferred_element_...  29.6 us
    all_gather x1, waiting for transfers between devices, per_device(): lax.all_gather(down_frozen_matrix, ('cuts', 'fsdp'), axis=1, tiled=True)  29.1 us
    dot_general x8, matrix products, matrix_product(): return jnp.dot(left, right, preferred_element_type=jnp.float32)  28.6 us
    all_gather x1, waiting for transfers between devices, per_device(): lax.all_gather(up_frozen_matrix, ('cuts', 'fsdp'), axis=0, tiled=True)  28.3 us
  transfers between devices with their start and end apart: 7, of which 7 were waited for; matrix products, arithmetic and copies ran while one was open for 13% of the time, Pallas kernels for 0%

commit v1 on v0

v1 whole, which is shorter than its diff:
```python
import functools
import math

import jax
import jax.numpy as jnp
from jax import lax
from jax.experimental import pallas as pl
from jax.experimental.pallas import tpu as pltpu
from jax.sharding import PartitionSpec as P

adapter_scaling = 0.5
VMEM_LIMIT = 56 * 1024 * 1024
ROW_TILE = 256
PIECES = 4
HALVES = 2
QUARTER_ORDER = ((3, 2, 1, 0), (0, 3, 2, 1), (3, 0, 1, 2), (0, 1, 2, 3))


def matrix_product(left, right):
    return jnp.dot(left, right, preferred_element_type=jnp.float32)


def contract_trailing_axis(left, right):
    return lax.dot_general(
        left, right, (((1,), (1,)), ((), ())), preferred_element_type=jnp.float32
    )


def contract_first(left, right):
    return lax.dot_general(
        left, right, (((0,), (0,)), ((), ())), preferred_element_type=jnp.float32
    )


def flip(array, axis, bit):
    size = lax.axis_size(axis)
    return lax.ppermute(array, axis, [(i, i ^ bit) for i in range(size)])


def forward_kernel(n_alias, layout, piece, position_ref, *refs):
    (tokens_ref, cotangent_ref, gate_low_ref, up_low_ref, back_low_ref) = refs[:5]
    (gate_out_ref, up_out_ref, down_in_ref) = refs[5:8]
    refs = refs[8:]
    blocks, refs = refs[: len(layout)], refs[len(layout) :]
    low_before_ref = refs[n_alias - 1] if n_alias else None
    refs = refs[n_alias:]
    (hidden_ref, gate_grad_ref, up_grad_ref, gate_full_ref, up_full_ref, low_ref) = refs[:6]
    weights, sems, out_sems = refs[6:]
    step = pl.program_id(0)
    columns = weights.shape[2]
    rows = blocks[0].shape[1]

    def block_copies():
        copies = []
        for number, (mask, offset) in enumerate(layout):
            block = blocks[number]
            place = pl.multiple_of(
                lax.bitwise_xor(position_ref[0], jnp.int32(mask)) * rows + offset, block.shape[1]
            )
            copies.append(
                pltpu.make_async_copy(
                    block, weights.at[:, pl.ds(place, block.shape[1]), :], sems.at[number]
                )
            )
        return copies

    def full_copies():
        return [
            pltpu.make_async_copy(
                weights.at[which],
                full.at[:, pl.ds(piece * columns, columns)],
                out_sems.at[which],
            )
            for which, full in enumerate((gate_full_ref, up_full_ref))
        ]

    @pl.when(step == 0)
    def _():
        for copy in block_copies():
            copy.start()
        for copy in block_copies():
            copy.wait()
        for copy in full_copies():
            copy.start()

    tokens = tokens_ref[...]
    gate = matrix_product(tokens, weights[0]) + adapter_scaling * matrix_product(
        gate_low_ref[...], gate_out_ref[...]
    )
    up = matrix_product(tokens, weights[1]) + adapter_scaling * matrix_product(
        up_low_ref[...], up_out_ref[...]
    )
    hidden_grad = matrix_product(
        cotangent_ref[...], weights[2]
    ) + adapter_scaling * contract_trailing_axis(back_low_ref[...], down_in_ref[...])
    sig = 1.0 / (1.0 + jnp.exp(-gate))
    gated = gate * sig
    hidden_ref[...] = (gated * up).astype(jnp.bfloat16)
    gate_grad = (hidden_grad * up * sig * (1.0 + gate * (1.0 - sig))).astype(jnp.bfloat16)
    up_grad = (hidden_grad * gated).astype(jnp.bfloat16)
    gate_grad_ref[...] = gate_grad
    up_grad_ref[...] = up_grad
    low = jnp.concatenate(
        [
            contract_trailing_axis(gate_grad, gate_out_ref[...]),
            contract_trailing_axis(up_grad, up_out_ref[...]),
        ],
        axis=1,
    )
    if low_before_ref is not None:
        low = low + low_before_ref[...]
    low_ref[...] = low

    @pl.when(step == pl.num_programs(0) - 1)
    def _():
        for copy in full_copies():
            copy.wait()


def forward_piece(
    piece, columns, position, tokens, cotangent, lows, factors, blocks, layout, before
):
    rows, width = tokens.shape
    rank = lows[0].shape[1]
    hidden_size = factors[0].shape[1]
    tile = min(ROW_TILE, rows)
    row_block = lambda last: pl.BlockSpec((tile, last), lambda i: (i, 0))
    anywhere = pl.BlockSpec(memory_space=pl.ANY)
    piece_block = pl.BlockSpec((tile, columns), lambda i: (i, piece))
    in_specs = (
        [pl.BlockSpec(memory_space=pltpu.SMEM)]
        + [row_block(width)] * 2
        + [row_block(rank)] * 3
        + [pl.BlockSpec((rank, columns), lambda i: (0, piece))] * 2
        + [pl.BlockSpec((columns, rank), lambda i: (piece, 0))]
        + [anywhere] * len(blocks)
    )
    args = [position, tokens, cotangent, *lows, *factors, *blocks]
    aliases = {}
    if before:
        for number, array in enumerate(before):
            aliases[len(args)] = number
            args.append(array)
            in_specs.append(anywhere if number < 5 else row_block(2 * rank))
    out_shape = (
        [jax.ShapeDtypeStruct((rows, hidden_size), jnp.bfloat16)] * 3
        + [jax.ShapeDtypeStruct((width, hidden_size), jnp.bfloat16)] * 2
        + [jax.ShapeDtypeStruct((rows, 2 * rank), jnp.float32)]
    )
    out_specs = [piece_block] * 3 + [anywhere] * 2 + [row_block(2 * rank)]
    return pl.pallas_call(
        functools.partial(forward_kernel, len(before), layout, piece),
        grid=(rows // tile,),
        in_specs=in_specs,
        out_specs=out_specs,
        out_shape=out_shape,
        scratch_shapes=[
            pltpu.VMEM((3, width, columns), jnp.bfloat16),
            pltpu.SemaphoreType.DMA((len(blocks),)),
            pltpu.SemaphoreType.DMA((2,)),
        ],
        input_output_aliases=aliases,
        compiler_params=pltpu.CompilerParams(vmem_limit_bytes=VMEM_LIMIT),
        cost_estimate=pl.CostEstimate(
            flops=6 * rows * width * columns,
            bytes_accessed=4 * rows * width + 10 * width * columns + 6 * rows * columns,
            transcendentals=rows * columns,
        ),
        name="forward_piece",
    )(*args)


def token_grad_kernel(quarter_ref, gate_grad_ref, up_grad_ref, gate_ref, up_ref, low_ref, factor_ref, out_ref):
    total = contract_trailing_axis(gate_grad_ref[...], gate_ref[...])
    total += contract_trailing_axis(up_grad_ref[...], up_ref[...])
    low = (adapter_scaling * low_ref[...]).astype(jnp.bfloat16)
    total += contract_trailing_axis(low, factor_ref[...])
    out_ref[...] = total.astype(out_ref.dtype)


def token_grad(quarter, half, kind, gate_grad, up_grad, gate, up, low, factor, columns):
    rows, hidden_size = gate_grad.shape
    part = rows // HALVES
    tile = min(ROW_TILE, part)
    steps = part // tile
    row_block = lambda last: pl.BlockSpec((tile, last), lambda i, q: (half * steps + i, 0))
    quarter_block = lambda last: pl.BlockSpec((columns, last), lambda i, q: (q[0], 0))
    return pl.pallas_call(
        token_grad_kernel,
        grid_spec=pltpu.PrefetchScalarGridSpec(
            num_scalar_prefetch=1,
            grid=(steps,),
            in_specs=[
                row_block(hidden_size),
                row_block(hidden_size),
                quarter_block(hidden_size),
                quarter_block(hidden_size),
                row_block(low.shape[1]),
                quarter_block(low.shape[1]),
            ],
            out_specs=pl.BlockSpec((tile, columns), lambda i, q: (i, 0)),
        ),
        out_shape=jax.ShapeDtypeStruct((part, columns), kind),
        compiler_params=pltpu.CompilerParams(vmem_limit_bytes=VMEM_LIMIT),
        cost_estimate=pl.CostEstimate(
            flops=4 * part * columns * hidden_size,
            bytes_accessed=4 * (part + columns) * hidden_size + 2 * part * columns,
            transcendentals=0,
        ),
        name="token_grad",
    )(quarter, gate_grad, up_grad, gate, up, low, factor)


def gather_blocks(own):
    size = lax.axis_size("fsdp")
    rows = own.shape[1]
    half = rows // 2
    whole = {0: own}
    upper, lower = {}, {}
    bits = [1 << number for number in range(size.bit_length() - 1)]
    for bit in bits:
        whole[bit] = flip(own, "fsdp", bit)
    for mask, block in whole.items():
        upper[mask], lower[mask] = block[:, :half], block[:, half:]
    for mask in range(size):
        if mask not in whole:
            high = 1 << (mask.bit_length() - 1)
            upper[mask] = flip(upper[mask ^ high], "fsdp", high)
    for mask in sorted(range(size), key=lambda m: bin(m).count("1")):
        if mask not in whole:
            low = mask & -mask
            lower[mask] = flip(lower[mask ^ low], "fsdp", low)
    blocks, layout = [], []
    for mask in range(size):
        if mask in whole:
            blocks.append(whole[mask])
            layout.append((mask, 0))
        else:
            blocks += [upper[mask], lower[mask]]
            layout += [(mask, 0), (mask, half)]
    other = [flip(block, "cuts", 1) for block in blocks]
    layout = layout + [(mask | size, offset) for mask, offset in layout]
    return blocks + other, tuple(layout)


def sum_over_plane(parts, cut, place):
    half = parts.shape[0] // 2
    parts = parts.reshape(2, half, *parts.shape[1:])
    mine = lax.dynamic_index_in_dim(parts, cut, 0, keepdims=False)
    parts = mine + flip(lax.dynamic_index_in_dim(parts, 1 - cut, 0, keepdims=False), "cuts", 1)
    bit = half // 2
    while bit:
        parts = parts.reshape(2, bit, *parts.shape[1:])
        up = (place // bit) % 2
        mine = lax.dynamic_index_in_dim(parts, up, 0, keepdims=False)
        parts = mine + flip(lax.dynamic_index_in_dim(parts, 1 - up, 0, keepdims=False), "fsdp", bit)
        bit //= 2
    return parts[0]


def copy_over_plane(rows, cut, place):
    bit = 1
    while bit < lax.axis_size("fsdp"):
        other = flip(rows, "fsdp", bit)
        up = (place // bit) % 2
        rows = jnp.where(
            up == 0, jnp.concatenate([rows, other]), jnp.concatenate([other, rows])
        )
        bit *= 2
    other = flip(rows, "cuts", 1)
    return jnp.where(cut == 0, jnp.concatenate([rows, other]), jnp.concatenate([other, rows]))


def sum_over_line(slots, place):
    first, second, third, last = slots
    shift = lambda array, pairs: lax.ppermute(array, "tp", pairs)
    plus = lambda a, b: (a.astype(jnp.float32) + b.astype(jnp.float32)).astype(jnp.bfloat16)
    came = shift(first, [(0, 1), (3, 2)])
    onward = plus(second, came)
    from_left = shift(onward, [(0, 1), (1, 2)])
    from_right = shift(onward, [(3, 2), (2, 1)])
    to_right = plus(jnp.where(place == 2, first, third), from_left)
    to_left = plus(jnp.where(place == 1, first, third), from_right)
    from_left = shift(to_right, [(0, 1), (1, 2), (2, 3)])
    from_right = shift(to_left, [(3, 2), (2, 1), (1, 0)])
    return (last + from_left.astype(jnp.float32) + from_right.astype(jnp.float32)).astype(
        jnp.bfloat16
    )


def per_device(
    tokens,
    cotangent,
    gate_frozen_matrix,
    up_frozen_matrix,
    down_frozen_matrix,
    gate_adapter_input_factor,
    up_adapter_input_factor,
    gate_adapter_output_factor,
    up_adapter_output_factor,
    down_adapter_input_factor,
    down_leave,
):
    groups = lax.axis_size(("cuts", "fsdp"))
    quarters = lax.axis_size("tp")
    cut = lax.axis_index("cuts")
    place = lax.axis_index("fsdp")
    quarter = lax.axis_index("tp")
    rows, width = tokens.shape
    hidden_size = gate_frozen_matrix.shape[1]
    rank = down_leave.shape[1]
    gradient_scaling = adapter_scaling / math.sqrt(rows * groups)
    position = lax.axis_index(("cuts", "fsdp")).astype(jnp.int32).reshape(1)

    columns = hidden_size // PIECES
    gathered = []
    for piece in range(PIECES):
        span = slice(piece * columns, (piece + 1) * columns)
        own = jnp.stack(
            [
                gate_frozen_matrix[:, span],
                up_frozen_matrix[:, span],
                down_frozen_matrix[span].T,
            ]
        )
        gathered.append(gather_blocks(own))

    lows = [
        matrix_product(tokens, gate_adapter_input_factor).astype(jnp.bfloat16),
        matrix_product(tokens, up_adapter_input_factor).astype(jnp.bfloat16),
        matrix_product(cotangent, down_leave).astype(jnp.bfloat16),
    ]
    factors = [gate_adapter_output_factor, up_adapter_output_factor, down_adapter_input_factor]
    state = ()
    for piece in range(PIECES):
        blocks, layout = gathered[piece]
        state = forward_piece(
            piece, columns, position, tokens, cotangent, lows, factors, blocks, layout, state
        )
    hidden, gate_grad, up_grad, gate_full, up_full, low = state

    input_factor = jnp.concatenate([gate_adapter_input_factor, up_adapter_input_factor], axis=1)
    order = jnp.asarray(QUARTER_ORDER, jnp.int32)[quarter]
    results = []
    for half in range(HALVES):
        slots = [
            token_grad(
                order[k : k + 1],
                half,
                jnp.float32 if k == quarters - 1 else jnp.bfloat16,
                gate_grad,
                up_grad,
                gate_full,
                up_full,
                low,
                input_factor,
                width // quarters,
            )
            for k in range(quarters)
        ]
        results.append(sum_over_line(slots, quarter))
    token_input_gradient = jnp.concatenate(results)

    down_low = matrix_product(hidden, down_adapter_input_factor).astype(jnp.bfloat16)
    narrow = gradient_scaling * jnp.concatenate(
        [
            contract_first(hidden, lows[2]),
            contract_first(gate_grad, lows[0]),
            contract_first(up_grad, lows[1]),
        ],
        axis=1,
    )
    wide = gradient_scaling * jnp.concatenate(
        [contract_first(tokens, low.astype(jnp.bfloat16)), contract_first(cotangent, down_low)],
        axis=1,
    )
    wide_rows = width // groups
    narrow_rows = hidden_size // groups
    both = jnp.concatenate(
        [
            wide.reshape(groups, wide_rows, 3 * rank),
            narrow.reshape(groups, narrow_rows, 3 * rank),
        ],
        axis=1,
    )
    both = sum_over_plane(both, cut, place)
    narrow_grads = copy_over_plane(both[wide_rows:], cut, place)
    wide_grads = both[:wide_rows]
    bit = quarters // 2
    while bit:
        parts = wide_grads.reshape(2, -1, 3 * rank)
        up = (quarter // bit) % 2
        mine = lax.dynamic_index_in_dim(parts, up, 0, keepdims=False)
        wide_grads = mine + flip(
            lax.dynamic_index_in_dim(parts, 1 - up, 0, keepdims=False), "tp", bit
        )
        bit //= 2
    return (token_input_gradient, wide_grads, narrow_grads)


def solution(mesh):
    in_specs = (
        P(("cuts", "fsdp"), None),
        P(("cuts", "fsdp"), None),
        P(("cuts", "fsdp"), "tp"),
        P(("cuts", "fsdp"), "tp"),
        P("tp", ("cuts", "fsdp")),
        P(),
        P(),
        P(None, "tp"),
        P(None, "tp"),
        P("tp", None),
        P(),
    )
    out_specs = (P(("cuts", "fsdp"), "tp"), P(("cuts", "fsdp", "tp"), None), P("tp", None))
    return jax.shard_map(
        per_device, mesh=mesh, in_specs=in_specs, out_specs=out_specs, check_vma=False
    )
```

time: 439 us -> 250 us (0.57)
  waiting for transfers between devices: 312 us -> 43.8 us
  Pallas kernels: 0 us -> 85.4 us
  starting transfers between devices: 0.28 us -> 65.7 us
  matrix products: 69 us -> 21 us
  blocking collectives: 33.8 us -> 0 us
  local copies, waits for them, and re-layouts: 6.14 us -> 20.6 us
  between operations: 14.4 us -> 1.78 us
  other arithmetic: 2.29 us -> 10 us
    reduce_scatter x2 -> x0, waiting for transfers between devices: 162 us -> none  [the longest x1 145 us: per_device(): lax.psum_scatter(partial_value, 'tp', scatter_dimension=1, tiled=True)]
    all_gather x3 -> x0, waiting for transfers between devices: 89.9 us -> none  [the longest x1 32.5 us: per_device(): lax.all_gather(gate_frozen_matrix, ('cuts', 'fsdp'), axis=0, tiled=True)]
    pallas_call x0 -> x12, Pallas kernels: none -> 85.4 us  [the longest x4 44.2 us: forward_piece(): pl.pallas_call(functools.partial(forward_kernel, len(before), layout, pie...]
    ppermute x0 -> x54, starting transfers between devices: none -> 65.7 us  [the longest x44 35.9 us: flip(): return lax.ppermute(array, axis, [(i, i ^ bit) for i in range(size)])]
    psum x2 -> x0, waiting for transfers between devices: 58.4 us -> none  [the longest x1 57.3 us: per_device(): narrow_grads = lax.psum(narrow_part, ('cuts', 'fsdp'))]
    ppermute x0 -> x54, waiting for transfers between devices: none -> 43.8 us  [the longest x44 38.5 us: flip(): return lax.ppermute(array, axis, [(i, i ^ bit) for i in range(size)])]
    psum x1 -> x0, blocking collectives: 33.8 us -> none  [per_device(): gate_sum, up_sum = lax.psum((gate_part, up_part), 'tp')]
    dot_general x8 -> x0, matrix products: 29.6 us -> none  [contract_trailing_axis(): lax.dot_general(left, right, (((1,), (1,)), ((), ())), preferred_element_...]
  transfers between devices with their start and end apart: 7 -> 54, of which waited for: 7 -> 14; matrix products, arithmetic and copies ran while one was open for 13% -> 10% of each run, Pallas kernels for 0% -> 30%
where the time goes in v1:
time: 250 us; the launch traced here: 248 us
  Pallas kernels  85.4 us (34%)
  starting transfers between devices  65.7 us (26%)
  waiting for transfers between devices  43.8 us (18%)
  matrix products  21 us (8%)
  local copies, waits for them, and re-layouts  20.6 us (8%)
  other arithmetic  10 us (4%)
    pallas_call x4, Pallas kernels, forward_piece(): pl.pallas_call(functools.partial(forward_kernel, len(before), layout, pie...  44.2 us
    pallas_call x8, Pallas kernels, token_grad(): pl.pallas_call(token_grad_kernel, grid_spec=pltpu.PrefetchScalarGridSpec(...  41.2 us
    ppermute x44, waiting for transfers between devices, flip(): return lax.ppermute(array, axis, [(i, i ^ bit) for i in range(size)])  38.5 us
    ppermute x44, starting transfers between devices, flip(): return lax.ppermute(array, axis, [(i, i ^ bit) for i in range(size)])  35.9 us
    ppermute x10, starting transfers between devices, sum_over_line(): shift = lambda array, pairs: lax.ppermute(array, 'tp', pairs)  29.8 us
    dot_general x5, matrix products, contract_first(): lax.dot_general(left, right, (((0,), (0,)), ((), ())), preferred_element_...  13 us
    unnamed x125, local copies, waits for them, and re-layouts  9.94 us
    dot_general x3, matrix products, matrix_product(): return jnp.dot(left, right, preferred_element_type=jnp.float32)  8.02 us
  transfers between devices with their start and end apart: 54, of which 14 were waited for; matrix products, arithmetic and copies ran while one was open for 10% of the time, Pallas kernels for 30%

profile of v1, /device:TPU:0, one launch (start us, length us, event | category | flops | bytes accessed | tf_op | source)
XLA Modules:
  0.0 248.2 jit_solution(4900381276639228329)
XLA Ops:
  0.6 1.2 fusion.12
  1.9 1.4 slice_bitcast_fusion
  3.4 3.0 %collective-permute-start.27 = (bf16[3,256,256]{2,1,0:T(8,128)(2,1)S(1)}, bf16[3,256,256]{2,1,0:T(8,128)(2,1)S(1)}, u32[]{:S(2)}, u32[]{:S(2)}) collective-permute-start(bf16[3,256,256]{2,1,0:T(8,128)(2,1)S(1)} %pad_maximum_fusion.5.refs_8_), channel_id=1, source_target_pairs={{0,4},{4,0},{8,12},{12,8},{1,5},{5,1},{9,13},{13,9},{2,6},{6,2},{1... | collective-permute-start | bytes 1179656 | tf_op jit(solution)/shard_map/ppermute | solution.py:37
  6.4 1.5 collective-permute-start.28
  9.0 7.3 %collective-permute-done.27.refs_9_ = bf16[3,256,256]{2,1,0:T(8,128)(2,1)S(1)} collective-permute-done((bf16[3,256,256]{2,1,0:T(8,128)(2,1)S(1)}, bf16[3,256,256]{2,1,0:T(8,128)(2,1)S(1)}, u32[]{:S(2)}, u32[]{:S(2)}) %collective-permute-start.27) | collective-permute-done | bytes 393248 | tf_op jit(solution)/shard_map/ppermute | solution.py:37
  16.3 2.1 collective-permute-start.9
  18.5 1.6 collective-permute-start.10
  20.8 4.1 %collective-permute-done.18.refs_9_ = bf16[3,256,256]{2,1,0:T(8,128)(2,1)} collective-permute-done((bf16[3,256,256]{2,1,0:T(8,128)(2,1)S(1)}, bf16[3,256,256]{2,1,0:T(8,128)(2,1)}, u32[]{:S(2)}, u32[]{:S(2)}) %collective-permute-start.18) | collective-permute-done | bytes 393248 | tf_op jit(solution)/shard_map/ppermute | solution.py:37
  24.8 2.1 collective-permute-start.1
  26.9 6.2 %collective-permute-done.9.refs_9_ = bf16[3,256,256]{2,1,0:T(8,128)(2,1)S(1)} collective-permute-done((bf16[3,256,256]{2,1,0:T(8,128)(2,1)S(1)}, bf16[3,256,256]{2,1,0:T(8,128)(2,1)S(1)}, u32[]{:S(2)}, u32[]{:S(2)}) %collective-permute-start.9) | collective-permute-done | bytes 393248 | tf_op jit(solution)/shard_map/ppermute | solution.py:37
  33.2 1.1 slice.133
  34.3 1.0 collective-permute-done.10.refs_10_
  35.3 1.5 collective-permute-start.29
  36.8 4.0 %collective-permute-done.refs_9_ = bf16[3,256,256]{2,1,0:T(8,128)(2,1)S(1)} collective-permute-done((bf16[3,256,256]{2,1,0:T(8,128)(2,1)S(1)}, bf16[3,256,256]{2,1,0:T(8,128)(2,1)S(1)}, u32[]{:S(2)}, u32[]{:S(2)}) %collective-permute-start) | collective-permute-done | bytes 393248 | tf_op jit(solution)/shard_map/ppermute | solution.py:37
  40.8 1.7 collective-permute-start.30
  42.5 1.2 collective-permute-done.1.refs_10_
  43.7 1.5 collective-permute-start.20
  45.2 4.1 %fusion.14.refs_2_ = bf16[1024,64]{1,0:T(8,128)(2,1)} fusion(bf16[1024,2048]{1,0:T(8,128)(2,1)} %refs_0_.7, bf16[2048,64]{0,1:T(8,128)(2,1)} %param.17), kind=kOutput, calls=%fused_computation.58 | convolution fusion | flops 268435456 | bytes 4587520 | tf_op jit(solution)/shard_map/dot_general | solution.py:20
  51.2 1.8 collective-permute-start.12
  53.1 1.5 collective-permute-start.2
  55.1 1.9 fusion.15.refs_3_
  57.1 1.4 collective-permute-done.21.refs_12_
  59.0 1.8 collective-permute-done.12.refs_12_
  61.4 1.6 collective-permute-done.3.refs_12_
  63.6 1.9 fusion.16.refs_4_
  65.7 2.0 copy.77
  67.7 2.0 copy.78
  73.8 11.3 %forward_piece.4 = (bf16[1024,1024]{1,0:T(8,128)(2,1)}, bf16[1024,1024]{1,0:T(8,128)(2,1)}, bf16[1024,1024]{1,0:T(8,128)(2,1)}, bf16[2048,1024]{1,0:T(8,128)(2,1...) custom-call(s32[1]{0:T(128)} %bitcast.1.position_ref, bf16[1024,2048]{1,0:T(8,128)(2,1)} %refs_0_.7, ...), custom_call_target="tpu_custom_call" | custom-call | flops 3221225472 | bytes 15204352 | tf_op jit(solution)/shard_map/forward_piece/pallas_call | solution.py:151
  86.3 11.0 %forward_piece.5 = (bf16[1024,1024]{1,0:T(8,128)(2,1)}, bf16[1024,1024]{1,0:T(8,128)(2,1)}, bf16[1024,1024]{1,0:T(8,128)(2,1)}, bf16[2048,1024]{1,0:T(8,128)(2,1...) custom-call(s32[1]{0:T(128)} %bitcast.1.position_ref, ...), custom_call_target="tpu_custom_call", output_to_operand_aliasing={{0}: (19, {}), {1}: (20, {}), {2}: (21, {}), {3}: (22, {}),... | custom-call | flops 3221225472 | bytes 15204352 | tf_op jit(solution)/shard_map/forward_piece/pallas_call | solution.py:151
  98.4 10.9 %forward_piece.6 = (bf16[1024,1024]{1,0:T(8,128)(2,1)}, bf16[1024,1024]{1,0:T(8,128)(2,1)}, bf16[1024,1024]{1,0:T(8,128)(2,1)}, bf16[2048,1024]{1,0:T(8,128)(2,1...) custom-call(s32[1]{0:T(128)} %bitcast.1.position_ref, ...), custom_call_target="tpu_custom_call", output_to_operand_aliasing={{0}: (19, {}), {1}: (20, {}), {2}: (21, {}), {3}: (22, {}),... | custom-call | flops 3221225472 | bytes 15204352 | tf_op jit(solution)/shard_map/forward_piece/pallas_call | solution.py:151
  110.5 11.0 %forward_piece.7 = (bf16[1024,1024]{1,0:T(8,128)(2,1)}, bf16[1024,1024]{1,0:T(8,128)(2,1)}, bf16[1024,1024]{1,0:T(8,128)(2,1)}, bf16[2048,1024]{1,0:T(8,128)(2,1...) custom-call(s32[1]{0:T(128)} %bitcast.1.position_ref, ...), custom_call_target="tpu_custom_call", output_to_operand_aliasing={{0}: (19, {}), {1}: (20, {}), {2}: (21, {}), {3}: (22, {}),... | custom-call | flops 3221225472 | bytes 15204352 | tf_op jit(solution)/shard_map/forward_piece/pallas_call | solution.py:151
  121.5 2.1 fusion.17
  123.6 5.3 %convolution_bitcast_fusion.1 = f32[2048,64]{0,1:T(8,128)} fusion(bf16[1024,2048]{1,0:T(8,128)(2,1)} %refs_1_.7, bf16[1024,1024]{1,0:T(8,128)(2,1)} %get-tuple-element.50, bf16[1024,64]{0,1:T(8,128)(2,1)S(1)} %copy-done.33), kind=kOutput, calls=%fused_computation.11 | convolution fusion | flops 402718720 | bytes 6946816 | tf_op jit(solution)/shard_map/dot_general | solution.py:30
  131.2 2.2 fusion.18
  134.3 2.9 %convolution_bitcast_fusion = f32[2048,128]{0,1:T(8,128)S(1)} fusion(bf16[1024,2048]{1,0:T(8,128)(2,1)} %refs_0_.7, f32[1024,128]{1,0:T(8,128)S(1)} %copy-done.5), kind=kOutput, calls=%fused_computation.10 | convolution fusion | flops 537001984 | bytes 5767168 | tf_op jit(solution)/shard_map/dot_general | solution.py:30
  141.7 1.1 pad_maximum_fusion.1.factor_ref
  142.8 5.3 %token_grad.9 = bf16[512,512]{1,0:T(8,128)(2,1)} custom-call(s32[1]{0:T(128)} %bitcast.18.quarter_ref, bf16[1024,1024]{1,0:T(8,128)(2,1)} %get-tuple-element.45.gate_grad_ref, bf16[1024,1024]{1,0:T(8,128)(2,1)} %get-tuple-element.46.up_grad_ref, bf16[2048,1024]{1,0:T(8,128)(2,1)} %get-tuple-element.47.gate_ref, bf16[2048,1024]{1,0:T(8,128)(2,1)} %get-tuple-element.48.up_ref, ...), custom_call_target="tpu_custom_call" | custom-call | flops 1073741824 | bytes 4718592 | tf_op jit(solution)/shard_map/token_grad/pallas_call | solution.py:188
  148.1 3.5 %collective-permute-start.36 = (bf16[512,512]{1,0:T(8,128)(2,1)}, bf16[512,512]{1,0:T(8,128)(2,1)S(1)}, u32[]{:S(2)}, u32[]{:S(2)}) collective-permute-start(bf16[512,512]{1,0:T(8,128)(2,1)} %token_grad.9), channel_id=1, source_target_pairs={{0,1},{3,2},{4,5},{7,6},{8,9},{11,10},{12,13},{15,14},{16,17},{19,... | collective-permute-start | bytes 1572872 | tf_op jit(solution)/shard_map/ppermute | solution.py:276
  151.6 5.1 %token_grad.13 = bf16[512,512]{1,0:T(8,128)(2,1)} custom-call(s32[1]{0:T(128)} %bitcast.18.quarter_ref, bf16[1024,1024]{1,0:T(8,128)(2,1)} %get-tuple-element.45.gate_grad_ref, bf16[1024,1024]{1,0:T(8,128)(2,1)} %get-tuple-element.46.up_grad_ref, bf16[2048,1024]{1,0:T(8,128)(2,1)} %get-tuple-element.47.gate_ref, ...), custom_call_target="tpu_custom_call" | custom-call | flops 1073741824 | bytes 4718592 | tf_op jit(solution)/shard_map/token_grad/pallas_call | solution.py:188
  156.7 1.3 collective-permute-start.41
  158.0 5.2 %token_grad.8 = f32[512,512]{1,0:T(8,128)} custom-call(s32[1]{0:T(128)} %bitcast.quarter_ref, bf16[1024,1024]{1,0:T(8,128)(2,1)} %get-tuple-element.45.gate_grad_ref, bf16[1024,1024]{1,0:T(8,128)(2,1)} %get-tuple-element.46.up_grad_ref, bf16[2048,1024]{1,0:T(8,128)(2,1)} %get-tuple-element.47.gate_ref, bf16[2048,1024]{1,0:T(8,128)(2,1)} %get-tuple-element.48.up_ref, ...), custom_call_target="tpu_custom_call" | custom-call | flops 1073741824 | bytes 4718592 | tf_op jit(solution)/shard_map/token_grad/pallas_call | solution.py:188
  163.2 5.2 %token_grad.12 = f32[512,512]{1,0:T(8,128)} custom-call(s32[1]{0:T(128)} %bitcast.quarter_ref, bf16[1024,1024]{1,0:T(8,128)(2,1)} %get-tuple-element.45.gate_grad_ref, bf16[1024,1024]{1,0:T(8,128)(2,1)} %get-tuple-element.46.up_grad_ref, bf16[2048,1024]{1,0:T(8,128)(2,1)} %get-tuple-element.47.gate_ref, bf16[2048,1024]{1,0:T(8,128)(2,1)} %get-tuple-element.48.up_ref, ...), custom_call_target="tpu_custom_call" | custom-call | flops 1073741824 | bytes 4718592 | tf_op jit(solution)/shard_map/token_grad/pallas_call | solution.py:188
  168.4 5.0 %token_grad.10 = bf16[512,512]{1,0:T(8,128)(2,1)} custom-call(s32[1]{0:T(128)} %bitcast.19.quarter_ref, bf16[1024,1024]{1,0:T(8,128)(2,1)} %get-tuple-element.45.gate_grad_ref, bf16[1024,1024]{1,0:T(8,128)(2,1)} %get-tuple-element.46.up_grad_ref, bf16[2048,1024]{1,0:T(8,128)(2,1)} %get-tuple-element.47.gate_ref, ...), custom_call_target="tpu_custom_call" | custom-call | flops 1073741824 | bytes 4718592 | tf_op jit(solution)/shard_map/token_grad/pallas_call | solution.py:188
  173.5 5.0 %token_grad.14 = bf16[512,512]{1,0:T(8,128)(2,1)} custom-call(s32[1]{0:T(128)} %bitcast.19.quarter_ref, bf16[1024,1024]{1,0:T(8,128)(2,1)} %get-tuple-element.45.gate_grad_ref, bf16[1024,1024]{1,0:T(8,128)(2,1)} %get-tuple-element.46.up_grad_ref, bf16[2048,1024]{1,0:T(8,128)(2,1)} %get-tuple-element.47.gate_ref, ...), custom_call_target="tpu_custom_call" | custom-call | flops 1073741824 | bytes 4718592 | tf_op jit(solution)/shard_map/token_grad/pallas_call | solution.py:188
  178.5 5.1 %token_grad.11 = bf16[512,512]{1,0:T(8,128)(2,1)} custom-call(s32[1]{0:T(128)} %bitcast.20.quarter_ref, bf16[1024,1024]{1,0:T(8,128)(2,1)} %get-tuple-element.45.gate_grad_ref, bf16[1024,1024]{1,0:T(8,128)(2,1)} %get-tuple-element.46.up_grad_ref, bf16[2048,1024]{1,0:T(8,128)(2,1)} %get-tuple-element.47.gate_ref, ...), custom_call_target="tpu_custom_call" | custom-call | flops 1073741824 | bytes 4718592 | tf_op jit(solution)/shard_map/token_grad/pallas_call | solution.py:188
  183.6 1.2 add_convert_fusion.7
  184.8 1.3 collective-permute-start.37
  187.6 5.2 %token_grad.15 = bf16[512,512]{1,0:T(8,128)(2,1)} custom-call(s32[1]{0:T(128)} %bitcast.20.quarter_ref, bf16[1024,1024]{1,0:T(8,128)(2,1)} %get-tuple-element.45.gate_grad_ref, bf16[1024,1024]{1,0:T(8,128)(2,1)} %get-tuple-element.46.up_grad_ref, bf16[2048,1024]{1,0:T(8,128)(2,1)} %get-tuple-element.47.gate_ref, ...), custom_call_target="tpu_custom_call" | custom-call | flops 1073741824 | bytes 4718592 | tf_op jit(solution)/shard_map/token_grad/pallas_call | solution.py:188
  192.8 1.2 add_convert_fusion.3
  194.0 4.1 %collective-permute-start.42 = (bf16[512,512]{1,0:T(8,128)(2,1)S(1)}, bf16[512,512]{1,0:T(8,128)(2,1)S(1)}, u32[]{:S(2)}, u32[]{:S(2)}) collective-permute-start(bf16[512,512]{1,0:T(8,128)(2,1)S(1)} %add_convert_fusion.3), channel_id=1, source_target_pairs={{0,1},{1,2},{4,5},{5,6},{8,9},{9,10},{12,13},{13,14},{16,17},{17,1... | collective-permute-start | bytes 1572872 | tf_op jit(solution)/shard_map/ppermute | solution.py:276
  199.2 6.4 %collective-permute-start.38 = (bf16[512,512]{1,0:T(8,128)(2,1)S(1)}, bf16[512,512]{1,0:T(8,128)(2,1)S(1)}, u32[]{:S(2)}, u32[]{:S(2)}) collective-permute-start(bf16[512,512]{1,0:T(8,128)(2,1)S(1)} %get-tuple-element.51), channel_id=1, source_target_pairs={{0,1},{1,2},{2,3},{4,5},{5,6},{6,7},{8,9},{9,10},{10,11},{12,13},{... | collective-permute-start | bytes 1572872 | tf_op jit(solution)/shard_map/ppermute | solution.py:276
  205.6 1.3 collective-permute-start.40
  207.7 2.8 %collective-permute-done.42 = bf16[512,512]{1,0:T(8,128)(2,1)S(1)} collective-permute-done((bf16[512,512]{1,0:T(8,128)(2,1)S(1)}, bf16[512,512]{1,0:T(8,128)(2,1)S(1)}, u32[]{:S(2)}, u32[]{:S(2)}) %collective-permute-start.42) | collective-permute-done | bytes 524320 | tf_op jit(solution)/shard_map/ppermute | solution.py:276
  210.5 1.3 add_convert_fusion.2
  211.8 9.0 %collective-permute-start.43 = (bf16[512,512]{1,0:T(8,128)(2,1)}, bf16[512,512]{1,0:T(8,128)(2,1)S(1)}, u32[]{:S(2)}, u32[]{:S(2)}) collective-permute-start(bf16[512,512]{1,0:T(8,128)(2,1)} %get-tuple-element.53), channel_id=1, source_target_pairs={{0,1},{1,2},{2,3},{4,5},{5,6},{6,7},{8,9},{9,10},{10,11},{12,13},{... | collective-permute-start | bytes 1572872 | tf_op jit(solution)/shard_map/ppermute | solution.py:276
  220.8 1.4 collective-permute-start.45
  223.9 5.6 %collective-permute-start.49 = (f32[128,192]{0,1:T(8,128)S(1)}, f32[128,192]{0,1:T(8,128)S(1)}, u32[]{:S(2)}, u32[]{:S(2)}) collective-permute-start(f32[128,192]{0,1:T(8,128)S(1)} %bitcast.94), channel_id=1, source_target_pairs={{0,2},{1,3},{2,0},{3,1},{4,6},{5,7},{6,4},{7,5},{8,10},{9,11},{10,... | collective-permute-start | bytes 294920 | tf_op jit(solution)/shard_map/ppermute | solution.py:37
  229.5 1.2 collective-permute-start.52
  230.7 2.2 collective-permute-done.43
  233.1 1.3 add_convert_fusion
  234.4 7.4 %collective-permute-done.49 = f32[128,192]{0,1:T(8,128)S(1)} collective-permute-done((f32[128,192]{0,1:T(8,128)S(1)}, f32[128,192]{0,1:T(8,128)S(1)}, u32[]{:S(2)}, u32[]{:S(2)}) %collective-permute-start.49) | collective-permute-done | bytes 98336 | tf_op jit(solution)/shard_map/ppermute | solution.py:37
  243.1 1.0 pad_maximum_fusion
  244.1 2.5 %collective-permute-done.50 = f32[64,192]{1,0:T(8,128)S(1)} collective-permute-done((f32[64,192]{1,0:T(8,128)S(1)}, f32[64,192]{1,0:T(8,128)S(1)}, u32[]{:S(2)}, u32[]{:S(2)}) %collective-permute-start.50) | collective-permute-done | bytes 49184 | tf_op jit(solution)/shard_map/ppermute | solution.py:37
  247.2 1.0 maximum_select_fusion
  (242 shorter events, 28.0 us)
Async XLA Ops:
  0.6 63.0 %copy-start = (bf16[2048,64]{0,1:T(8,128)(2,1)S(1)}, bf16[2048,64]{0,1:T(8,128)(2,1)}, u32[]{:S(2)}) copy-start(bf16[2048,64]{0,1:T(8,128)(2,1)} %param.22) | copy-start | bytes 786436
  3.4 30.9 %copy-start.18 = (bf16[3,256,256]{2,1,0:T(8,128)(2,1)}, bf16[3,256,256]{2,1,0:T(8,128)(2,1)S(1)}, u32[]{:S(2)}) copy-start(bf16[3,256,256]{2,1,0:T(8,128)(2,1)S(1)} %pad_maximum_fusion.5.refs_8_) | copy-start | bytes 1179652
  3.4 12.9 %collective-permute-start.27 = (bf16[3,256,256]{2,1,0:T(8,128)(2,1)S(1)}, bf16[3,256,256]{2,1,0:T(8,128)(2,1)S(1)}, u32[]{:S(2)}, u32[]{:S(2)}) collective-permute-start(bf16[3,256,256]{2,1,0:T(8,128)(2,1)S(1)} %pad_maximum_fusion.5.refs_8_), channel_id=1, source_target_pairs={{0,4},{4,0},{8,12},{12,8},{1,5},{5,1},{9,13},{13,9},{2,6},{6,2},{1... | collective-permute-start | bytes 1179656 | tf_op jit(solution)/shard_map/ppermute | solution.py:37
  6.4 12.1 %collective-permute-start.28 = (bf16[3,256,256]{2,1,0:T(8,128)(2,1)S(1)}, bf16[3,256,256]{2,1,0:T(8,128)(2,1)S(1)}, u32[]{:S(2)}, u32[]{:S(2)}) collective-permute-start(bf16[3,256,256]{2,1,0:T(8,128)(2,1)S(1)} %pad_maximum_fusion.5.refs_8_), channel_id=1, source_target_pairs={{0,8},{4,12},{8,0},{12,4},{1,9},{5,13},{9,1},{13,5},{2,10},{6,14},... | collective-permute-start | bytes 1179656 | tf_op jit(solution)/shard_map/ppermute | solution.py:37
  7.9 12.2 %collective-permute-start.31 = (bf16[3,256,256]{2,1,0:T(8,128)(2,1)S(1)}, bf16[3,256,256]{2,1,0:T(8,128)(2,1)S(1)}, u32[]{:S(2)}, u32[]{:S(2)}) collective-permute-start(bf16[3,256,256]{2,1,0:T(8,128)(2,1)S(1)} %pad_maximum_fusion.5.refs_8_), channel_id=1, source_target_pairs={{0,16},{16,0},{1,17},{17,1},{2,18},{18,2},{3,19},{19,3},{4,20},{20... | collective-permute-start | bytes 1179656 | tf_op jit(solution)/shard_map/ppermute | solution.py:37
  8.1 41.3 %copy-start.21 = (bf16[3,256,256]{2,1,0:T(8,128)(2,1)}, bf16[3,256,256]{2,1,0:T(8,128)(2,1)S(1)}, u32[]{:S(2)}) copy-start(bf16[3,256,256]{2,1,0:T(8,128)(2,1)S(1)} %pad_maximum_fusion.4.refs_8_) | copy-start | bytes 1179652
  8.1 16.8 %collective-permute-start.18 = (bf16[3,256,256]{2,1,0:T(8,128)(2,1)S(1)}, bf16[3,256,256]{2,1,0:T(8,128)(2,1)}, u32[]{:S(2)}, u32[]{:S(2)}) collective-permute-start(bf16[3,256,256]{2,1,0:T(8,128)(2,1)S(1)} %pad_maximum_fusion.4.refs_8_), channel_id=1, source_target_pairs={{0,4},{4,0},{8,12},{12,8},{1,5},{5,1},{9,13},{13,9},{2,6},{6,2},{1... | collective-permute-start | bytes 1179656 | tf_op jit(solution)/shard_map/ppermute | solution.py:37
  8.7 18.3 %collective-permute-start.19 = (bf16[3,256,256]{2,1,0:T(8,128)(2,1)S(1)}, bf16[3,256,256]{2,1,0:T(8,128)(2,1)}, u32[]{:S(2)}, u32[]{:S(2)}) collective-permute-start(bf16[3,256,256]{2,1,0:T(8,128)(2,1)S(1)} %pad_maximum_fusion.4.refs_8_), channel_id=1, source_target_pairs={{0,8},{4,12},{8,0},{12,4},{1,9},{5,13},{9,1},{13,5},{2,10},{6,14},... | collective-permute-start | bytes 1179656 | tf_op jit(solution)/shard_map/ppermute | solution.py:37
  9.0 40.4 %copy-start.20 = (bf16[3,256,256]{2,1,0:T(8,128)(2,1)}, bf16[3,256,256]{2,1,0:T(8,128)(2,1)S(1)}, u32[]{:S(2)}) copy-start(bf16[3,256,256]{2,1,0:T(8,128)(2,1)S(1)} %pad_maximum_fusion.3.refs_8_) | copy-start | bytes 1179652
  16.3 42.1 %copy-start.25 = (bf16[3,256,256]{2,1,0:T(8,128)(2,1)}, bf16[3,256,256]{2,1,0:T(8,128)(2,1)S(1)}, u32[]{:S(2)}) copy-start(bf16[3,256,256]{2,1,0:T(8,128)(2,1)S(1)} %collective-permute-done.27.refs_9_) | copy-start | bytes 1179652
  16.3 16.9 %collective-permute-start.9 = (bf16[3,256,256]{2,1,0:T(8,128)(2,1)S(1)}, bf16[3,256,256]{2,1,0:T(8,128)(2,1)S(1)}, u32[]{:S(2)}, u32[]{:S(2)}) collective-permute-start(bf16[3,256,256]{2,1,0:T(8,128)(2,1)S(1)} %pad_maximum_fusion.3.refs_8_), channel_id=1, source_target_pairs={{0,4},{4,0},{8,12},{12,8},{1,5},{5,1},{9,13},{13,9},{2,6},{6,2},{1... | collective-permute-start | bytes 1179656 | tf_op jit(solution)/shard_map/ppermute | solution.py:37
  18.4 66.7 %copy-start.19 = (bf16[3,256,256]{2,1,0:T(8,128)(2,1)}, bf16[3,256,256]{2,1,0:T(8,128)(2,1)S(1)}, u32[]{:S(2)}) copy-start(bf16[3,256,256]{2,1,0:T(8,128)(2,1)S(1)} %pad_maximum_fusion.2.refs_8_) | copy-start | bytes 1179652
  18.4 40.0 %copy-start.26 = (bf16[3,256,256]{2,1,0:T(8,128)(2,1)}, bf16[3,256,256]{2,1,0:T(8,128)(2,1)S(1)}, u32[]{:S(2)}) copy-start(bf16[3,256,256]{2,1,0:T(8,128)(2,1)S(1)} %collective-permute-done.28.refs_10_) | copy-start | bytes 1179652
  18.5 16.8 %collective-permute-start.10 = (bf16[3,256,256]{2,1,0:T(8,128)(2,1)S(1)}, bf16[3,256,256]{2,1,0:T(8,128)(2,1)S(1)}, u32[]{:S(2)}, u32[]{:S(2)}) collective-permute-start(bf16[3,256,256]{2,1,0:T(8,128)(2,1)S(1)} %pad_maximum_fusion.3.refs_8_), channel_id=1, source_target_pairs={{0,8},{4,12},{8,0},{12,4},{1,9},{5,13},{9,1},{13,5},{2,10},{6,14},... | collective-permute-start | bytes 1179656 | tf_op jit(solution)/shard_map/ppermute | solution.py:37
  20.0 20.7 %collective-permute-start = (bf16[3,256,256]{2,1,0:T(8,128)(2,1)S(1)}, bf16[3,256,256]{2,1,0:T(8,128)(2,1)S(1)}, u32[]{:S(2)}, u32[]{:S(2)}) collective-permute-start(bf16[3,256,256]{2,1,0:T(8,128)(2,1)S(1)} %pad_maximum_fusion.2.refs_8_), channel_id=1, source_target_pairs={{0,4},{4,0},{8,12},{12,8},{1,5},{5,1},{9,13},{13,9},{2,6},{6,2},{1... | collective-permute-start | bytes 1179656 | tf_op jit(solution)/shard_map/ppermute | solution.py:37
  24.8 18.8 %collective-permute-start.1 = (bf16[3,256,256]{2,1,0:T(8,128)(2,1)S(1)}, bf16[3,256,256]{2,1,0:T(8,128)(2,1)S(1)}, u32[]{:S(2)}, u32[]{:S(2)}) collective-permute-start(bf16[3,256,256]{2,1,0:T(8,128)(2,1)S(1)} %pad_maximum_fusion.2.refs_8_), channel_id=1, source_target_pairs={{0,8},{4,12},{8,0},{12,4},{1,9},{5,13},{9,1},{13,5},{2,10},{6,14},... | collective-permute-start | bytes 1179656 | tf_op jit(solution)/shard_map/ppermute | solution.py:37
  26.9 23.5 %collective-permute-start.22 = (bf16[3,256,256]{2,1,0:T(8,128)(2,1)S(1)}, bf16[3,256,256]{2,1,0:T(8,128)(2,1)S(1)}, u32[]{:S(2)}, u32[]{:S(2)}) collective-permute-start(bf16[3,256,256]{2,1,0:T(8,128)(2,1)S(1)} %pad_maximum_fusion.4.refs_8_), channel_id=1, source_target_pairs={{0,16},{16,0},{1,17},{17,1},{2,18},{18,2},{3,19},{19,3},{4,20},{20... | collective-permute-start | bytes 1179656 | tf_op jit(solution)/shard_map/ppermute | solution.py:37
  33.2 17.9 %collective-permute-start.13 = (bf16[3,256,256]{2,1,0:T(8,128)(2,1)S(1)}, bf16[3,256,256]{2,1,0:T(8,128)(2,1)S(1)}, u32[]{:S(2)}, u32[]{:S(2)}) collective-permute-start(bf16[3,256,256]{2,1,0:T(8,128)(2,1)S(1)} %pad_maximum_fusion.3.refs_8_), channel_id=1, source_target_pairs={{0,16},{16,0},{1,17},{17,1},{2,18},{18,2},{3,19},{19,3},{4,20},{20... | collective-permute-start | bytes 1179656 | tf_op jit(solution)/shard_map/ppermute | solution.py:37
  34.3 20.8 %copy-start.4 = (bf16[1024,2048]{1,0:T(8,128)(2,1)S(1)}, bf16[1024,2048]{1,0:T(8,128)(2,1)}, u32[]{:S(2)}) copy-start(bf16[1024,2048]{1,0:T(8,128)(2,1)} %refs_0_.7) | copy-start | bytes 12582916
  35.3 15.9 %collective-permute-start.29 = (bf16[3,128,256]{2,1,0:T(8,128)(2,1)S(1)}, bf16[3,128,256]{2,1,0:T(8,128)(2,1)}, u32[]{:S(2)}, u32[]{:S(2)}) collective-permute-start(bf16[3,128,256]{2,1,0:T(8,128)(2,1)S(1)} %slice.135), channel_id=1, source_target_pairs={{0,8},{4,12},{8,0},{12,4},{1,9},{5,13},{9,1},{13,5},{2,10},{6,14},... | collective-permute-start | bytes 589832 | tf_op jit(solution)/shard_map/ppermute | solution.py:37
  40.8 44.9 %copy-start.27 = (bf16[3,256,256]{2,1,0:T(8,128)(2,1)}, bf16[3,256,256]{2,1,0:T(8,128)(2,1)S(1)}, u32[]{:S(2)}) copy-start(bf16[3,256,256]{2,1,0:T(8,128)(2,1)S(1)} %collective-permute-done.refs_9_) | copy-start | bytes 1179652
  40.8 12.3 %collective-permute-start.30 = (bf16[3,128,256]{2,1,0:T(8,128)(2,1)S(1)}, bf16[3,128,256]{2,1,0:T(8,128)(2,1)}, u32[]{:S(2)}, u32[]{:S(2)}) collective-permute-start(bf16[3,128,256]{2,1,0:T(8,128)(2,1)S(1)} %slice.136), channel_id=1, source_target_pairs={{0,4},{4,0},{8,12},{12,8},{1,5},{5,1},{9,13},{13,9},{2,6},{6,2},{1... | collective-permute-start | bytes 589832 | tf_op jit(solution)/shard_map/ppermute | solution.py:37
  43.7 42.1 %copy-start.28 = (bf16[3,256,256]{2,1,0:T(8,128)(2,1)}, bf16[3,256,256]{2,1,0:T(8,128)(2,1)S(1)}, u32[]{:S(2)}) copy-start(bf16[3,256,256]{2,1,0:T(8,128)(2,1)S(1)} %collective-permute-done.1.refs_10_) | copy-start | bytes 1179652
  43.7 10.9 %collective-permute-start.20 = (bf16[3,128,256]{2,1,0:T(8,128)(2,1)S(1)}, bf16[3,128,256]{2,1,0:T(8,128)(2,1)S(1)}, u32[]{:S(2)}, u32[]{:S(2)}) collective-permute-start(bf16[3,128,256]{2,1,0:T(8,128)(2,1)S(1)} %slice.133), channel_id=1, source_target_pairs={{0,8},{4,12},{8,0},{12,4},{1,9},{5,13},{9,1},{13,5},{2,10},{6,14},... | collective-permute-start | bytes 589832 | tf_op jit(solution)/shard_map/ppermute | solution.py:37
  50.4 8.0 %collective-permute-start.21 = (bf16[3,128,256]{2,1,0:T(8,128)(2,1)S(1)}, bf16[3,128,256]{2,1,0:T(8,128)(2,1)}, u32[]{:S(2)}, u32[]{:S(2)}) collective-permute-start(bf16[3,128,256]{2,1,0:T(8,128)(2,1)S(1)} %slice.134), channel_id=1, source_target_pairs={{0,4},{4,0},{8,12},{12,8},{1,5},{5,1},{9,13},{13,9},{2,6},{6,2},{1... | collective-permute-start | bytes 589832 | tf_op jit(solution)/shard_map/ppermute | solution.py:37
  51.1 7.4 %collective-permute-start.11 = (bf16[3,128,256]{2,1,0:T(8,128)(2,1)S(1)}, bf16[3,128,256]{2,1,0:T(8,128)(2,1)S(1)}, u32[]{:S(2)}, u32[]{:S(2)}) collective-permute-start(bf16[3,128,256]{2,1,0:T(8,128)(2,1)S(1)} %slice.131), channel_id=1, source_target_pairs={{0,8},{4,12},{8,0},{12,4},{1,9},{5,13},{9,1},{13,5},{2,10},{6,14},... | collective-permute-start | bytes 589832 | tf_op jit(solution)/shard_map/ppermute | solution.py:37
  51.2 9.7 %collective-permute-start.12 = (bf16[3,128,256]{2,1,0:T(8,128)(2,1)S(1)}, bf16[3,128,256]{2,1,0:T(8,128)(2,1)S(1)}, u32[]{:S(2)}, u32[]{:S(2)}) collective-permute-start(bf16[3,128,256]{2,1,0:T(8,128)(2,1)S(1)} %slice.132), channel_id=1, source_target_pairs={{0,4},{4,0},{8,12},{12,8},{1,5},{5,1},{9,13},{13,9},{2,6},{6,2},{1... | collective-permute-start | bytes 589832 | tf_op jit(solution)/shard_map/ppermute | solution.py:37
  53.1 7.8 %collective-permute-start.2 = (bf16[3,128,256]{2,1,0:T(8,128)(2,1)S(1)}, bf16[3,128,256]{2,1,0:T(8,128)(2,1)S(1)}, u32[]{:S(2)}, u32[]{:S(2)}) collective-permute-start(bf16[3,128,256]{2,1,0:T(8,128)(2,1)S(1)} %slice.129), channel_id=1, source_target_pairs={{0,8},{4,12},{8,0},{12,4},{1,9},{5,13},{9,1},{13,5},{2,10},{6,14},... | collective-permute-start | bytes 589832 | tf_op jit(solution)/shard_map/ppermute | solution.py:37
  54.6 8.4 %collective-permute-start.3 = (bf16[3,128,256]{2,1,0:T(8,128)(2,1)S(1)}, bf16[3,128,256]{2,1,0:T(8,128)(2,1)S(1)}, u32[]{:S(2)}, u32[]{:S(2)}) collective-permute-start(bf16[3,128,256]{2,1,0:T(8,128)(2,1)S(1)} %slice.130), channel_id=1, source_target_pairs={{0,4},{4,0},{8,12},{12,8},{1,5},{5,1},{9,13},{13,9},{2,6},{6,2},{1... | collective-permute-start | bytes 589832 | tf_op jit(solution)/shard_map/ppermute | solution.py:37
  58.5 13.3 %collective-permute-start.32 = (bf16[3,256,256]{2,1,0:T(8,128)(2,1)S(1)}, bf16[3,256,256]{2,1,0:T(8,128)(2,1)S(1)}, u32[]{:S(2)}, u32[]{:S(2)}) collective-permute-start(bf16[3,256,256]{2,1,0:T(8,128)(2,1)S(1)} %collective-permute-done.27.refs_9_), channel_id=1, source_target_pairs={{0,16},{16,0},{1,17},{17,1},{2,18},{18,2},{3,19},{19,3},{4,20},{20... | collective-permute-start | bytes 1179656 | tf_op jit(solution)/shard_map/ppermute | solution.py:37
  58.5 14.1 %collective-permute-start.33 = (bf16[3,256,256]{2,1,0:T(8,128)(2,1)S(1)}, bf16[3,256,256]{2,1,0:T(8,128)(2,1)}, u32[]{:S(2)}, u32[]{:S(2)}) collective-permute-start(bf16[3,256,256]{2,1,0:T(8,128)(2,1)S(1)} %collective-permute-done.28.refs_10_), channel_id=1, source_target_pairs={{0,16},{16,0},{1,17},{17,1},{2,18},{18,2},{3,19},{19,3},{4,20},{20... | collective-permute-start | bytes 1179656 | tf_op jit(solution)/shard_map/ppermute | solution.py:37
  60.9 12.9 %collective-permute-start.23 = (bf16[3,256,256]{2,1,0:T(8,128)(2,1)}, bf16[3,256,256]{2,1,0:T(8,128)(2,1)}, u32[]{:S(2)}, u32[]{:S(2)}) collective-permute-start(bf16[3,256,256]{2,1,0:T(8,128)(2,1)} %collective-permute-done.18.refs_9_), channel_id=1, source_target_pairs={{0,16},{16,0},{1,17},{17,1},{2,18},{18,2},{3,19},{19,3},{4,20},{20... | collective-permute-start | bytes 1179656 | tf_op jit(solution)/shard_map/ppermute | solution.py:37
  60.9 9.7 %collective-permute-start.34 = (bf16[3,128,256]{2,1,0:T(8,128)(2,1)}, bf16[3,128,256]{2,1,0:T(8,128)(2,1)}, u32[]{:S(2)}, u32[]{:S(2)}) collective-permute-start(bf16[3,128,256]{2,1,0:T(8,128)(2,1)} %collective-permute-done.29.refs_11_), channel_id=1, source_target_pairs={{0,16},{16,0},{1,17},{17,1},{2,18},{18,2},{3,19},{19,3},{4,20},{20... | collective-permute-start | bytes 589832 | tf_op jit(solution)/shard_map/ppermute | solution.py:37
  63.0 7.6 %collective-permute-start.35 = (bf16[3,128,256]{2,1,0:T(8,128)(2,1)}, bf16[3,128,256]{2,1,0:T(8,128)(2,1)}, u32[]{:S(2)}, u32[]{:S(2)}) collective-permute-start(bf16[3,128,256]{2,1,0:T(8,128)(2,1)} %collective-permute-done.30.refs_12_), channel_id=1, source_target_pairs={{0,16},{16,0},{1,17},{17,1},{2,18},{18,2},{3,19},{19,3},{4,20},{20... | collective-permute-start | bytes 589832 | tf_op jit(solution)/shard_map/ppermute | solution.py:37
  70.6 2.5 %collective-permute-start.25 = (bf16[3,128,256]{2,1,0:T(8,128)(2,1)}, bf16[3,128,256]{2,1,0:T(8,128)(2,1)S(1)}, u32[]{:S(2)}, u32[]{:S(2)}) collective-permute-start(bf16[3,128,256]{2,1,0:T(8,128)(2,1)} %copy-done.52), channel_id=1, source_target_pairs={{0,16},{16,0},{1,17},{17,1},{2,18},{18,2},{3,19},{19,3},{4,20},{20... | collective-permute-start | bytes 589832 | tf_op jit(solution)/shard_map/ppermute | solution.py:37
  70.6 2.6 %collective-permute-start.26 = (bf16[3,128,256]{2,1,0:T(8,128)(2,1)}, bf16[3,128,256]{2,1,0:T(8,128)(2,1)S(1)}, u32[]{:S(2)}, u32[]{:S(2)}) collective-permute-start(bf16[3,128,256]{2,1,0:T(8,128)(2,1)} %collective-permute-done.21.refs_12_), channel_id=1, source_target_pairs={{0,16},{16,0},{1,17},{17,1},{2,18},{18,2},{3,19},{19,3},{4,20},{20... | collective-permute-start | bytes 589832 | tf_op jit(solution)/shard_map/ppermute | solution.py:37
  71.8 13.3 %collective-permute-start.24 = (bf16[3,256,256]{2,1,0:T(8,128)(2,1)}, bf16[3,256,256]{2,1,0:T(8,128)(2,1)S(1)}, u32[]{:S(2)}, u32[]{:S(2)}) collective-permute-start(bf16[3,256,256]{2,1,0:T(8,128)(2,1)} %collective-permute-done.19.refs_10_), channel_id=1, source_target_pairs={{0,16},{16,0},{1,17},{17,1},{2,18},{18,2},{3,19},{19,3},{4,20},{20... | collective-permute-start | bytes 1179656 | tf_op jit(solution)/shard_map/ppermute | solution.py:37
  72.6 24.7 %collective-permute-start.14 = (bf16[3,256,256]{2,1,0:T(8,128)(2,1)S(1)}, bf16[3,256,256]{2,1,0:T(8,128)(2,1)S(1)}, u32[]{:S(2)}, u32[]{:S(2)}) collective-permute-start(bf16[3,256,256]{2,1,0:T(8,128)(2,1)S(1)} %copy-done.30), channel_id=1, source_target_pairs={{0,16},{16,0},{1,17},{17,1},{2,18},{18,2},{3,19},{19,3},{4,20},{20... | collective-permute-start | bytes 1179656 | tf_op jit(solution)/shard_map/ppermute | solution.py:37
  73.1 24.5 %collective-permute-start.15 = (bf16[3,256,256]{2,1,0:T(8,128)(2,1)S(1)}, bf16[3,256,256]{2,1,0:T(8,128)(2,1)S(1)}, u32[]{:S(2)}, u32[]{:S(2)}) collective-permute-start(bf16[3,256,256]{2,1,0:T(8,128)(2,1)S(1)} %copy-done.32), channel_id=1, source_target_pairs={{0,16},{16,0},{1,17},{17,1},{2,18},{18,2},{3,19},{19,3},{4,20},{20... | collective-permute-start | bytes 1179656 | tf_op jit(solution)/shard_map/ppermute | solution.py:37
  73.2 12.4 %collective-permute-start.16 = (bf16[3,128,256]{2,1,0:T(8,128)(2,1)S(1)}, bf16[3,128,256]{2,1,0:T(8,128)(2,1)S(1)}, u32[]{:S(2)}, u32[]{:S(2)}) collective-permute-start(bf16[3,128,256]{2,1,0:T(8,128)(2,1)S(1)} %copy-done.50), channel_id=1, source_target_pairs={{0,16},{16,0},{1,17},{17,1},{2,18},{18,2},{3,19},{19,3},{4,20},{20... | collective-permute-start | bytes 589832 | tf_op jit(solution)/shard_map/ppermute | solution.py:37
  73.7 12.1 %collective-permute-start.17 = (bf16[3,128,256]{2,1,0:T(8,128)(2,1)}, bf16[3,128,256]{2,1,0:T(8,128)(2,1)S(1)}, u32[]{:S(2)}, u32[]{:S(2)}) collective-permute-start(bf16[3,128,256]{2,1,0:T(8,128)(2,1)} %copy-done.51), channel_id=1, source_target_pairs={{0,16},{16,0},{1,17},{17,1},{2,18},{18,2},{3,19},{19,3},{4,20},{20... | collective-permute-start | bytes 589832 | tf_op jit(solution)/shard_map/ppermute | solution.py:37
  85.1 24.2 %collective-permute-start.4 = (bf16[3,256,256]{2,1,0:T(8,128)(2,1)S(1)}, bf16[3,256,256]{2,1,0:T(8,128)(2,1)S(1)}, u32[]{:S(2)}, u32[]{:S(2)}) collective-permute-start(bf16[3,256,256]{2,1,0:T(8,128)(2,1)S(1)} %pad_maximum_fusion.2.refs_8_), channel_id=1, source_target_pairs={{0,16},{16,0},{1,17},{17,1},{2,18},{18,2},{3,19},{19,3},{4,20},{20... | collective-permute-start | bytes 1179656 | tf_op jit(solution)/shard_map/ppermute | solution.py:37
  85.6 23.7 %collective-permute-start.5 = (bf16[3,256,256]{2,1,0:T(8,128)(2,1)S(1)}, bf16[3,256,256]{2,1,0:T(8,128)(2,1)S(1)}, u32[]{:S(2)}, u32[]{:S(2)}) collective-permute-start(bf16[3,256,256]{2,1,0:T(8,128)(2,1)S(1)} %collective-permute-done.refs_9_), channel_id=1, source_target_pairs={{0,16},{16,0},{1,17},{17,1},{2,18},{18,2},{3,19},{19,3},{4,20},{20... | collective-permute-start | bytes 1179656 | tf_op jit(solution)/shard_map/ppermute | solution.py:37
  85.8 23.6 %collective-permute-start.6 = (bf16[3,256,256]{2,1,0:T(8,128)(2,1)S(1)}, bf16[3,256,256]{2,1,0:T(8,128)(2,1)S(1)}, u32[]{:S(2)}, u32[]{:S(2)}) collective-permute-start(bf16[3,256,256]{2,1,0:T(8,128)(2,1)S(1)} %collective-permute-done.1.refs_10_), channel_id=1, source_target_pairs={{0,16},{16,0},{1,17},{17,1},{2,18},{18,2},{3,19},{19,3},{4,20},{20... | collective-permute-start | bytes 1179656 | tf_op jit(solution)/shard_map/ppermute | solution.py:37
  97.3 12.0 %collective-permute-start.7 = (bf16[3,128,256]{2,1,0:T(8,128)(2,1)S(1)}, bf16[3,128,256]{2,1,0:T(8,128)(2,1)S(1)}, u32[]{:S(2)}, u32[]{:S(2)}) collective-permute-start(bf16[3,128,256]{2,1,0:T(8,128)(2,1)S(1)} %copy-done.46), channel_id=1, source_target_pairs={{0,16},{16,0},{1,17},{17,1},{2,18},{18,2},{3,19},{19,3},{4,20},{20... | collective-permute-start | bytes 589832 | tf_op jit(solution)/shard_map/ppermute | solution.py:37
  97.6 11.7 %collective-permute-start.8 = (bf16[3,128,256]{2,1,0:T(8,128)(2,1)S(1)}, bf16[3,128,256]{2,1,0:T(8,128)(2,1)S(1)}, u32[]{:S(2)}, u32[]{:S(2)}) collective-permute-start(bf16[3,128,256]{2,1,0:T(8,128)(2,1)S(1)} %copy-done.48), channel_id=1, source_target_pairs={{0,16},{16,0},{1,17},{17,1},{2,18},{18,2},{3,19},{19,3},{4,20},{20... | collective-permute-start | bytes 589832 | tf_op jit(solution)/shard_map/ppermute | solution.py:37
  140.6 46.2 %collective-permute-start.46 = (f32[4,384,192]{1,2,0:T(8,128)S(1)}, f32[4,384,192]{1,2,0:T(8,128)S(1)}, u32[]{:S(2)}, u32[]{:S(2)}) collective-permute-start(f32[4,384,192]{1,2,0:T(8,128)S(1)} %fusion.7), channel_id=1, source_target_pairs={{0,16},{16,0},{1,17},{17,1},{2,18},{18,2},{3,19},{19,3},{4,20},{20... | collective-permute-start | bytes 3538952 | tf_op jit(solution)/shard_map/ppermute | solution.py:37
  148.1 35.5 %collective-permute-start.36 = (bf16[512,512]{1,0:T(8,128)(2,1)}, bf16[512,512]{1,0:T(8,128)(2,1)S(1)}, u32[]{:S(2)}, u32[]{:S(2)}) collective-permute-start(bf16[512,512]{1,0:T(8,128)(2,1)} %token_grad.9), channel_id=1, source_target_pairs={{0,1},{3,2},{4,5},{7,6},{8,9},{11,10},{12,13},{15,14},{16,17},{19,... | collective-permute-start | bytes 1572872 | tf_op jit(solution)/shard_map/ppermute | solution.py:276
  156.7 36.1 %collective-permute-start.41 = (bf16[512,512]{1,0:T(8,128)(2,1)}, bf16[512,512]{1,0:T(8,128)(2,1)S(1)}, u32[]{:S(2)}, u32[]{:S(2)}) collective-permute-start(bf16[512,512]{1,0:T(8,128)(2,1)} %token_grad.13), channel_id=1, source_target_pairs={{0,1},{3,2},{4,5},{7,6},{8,9},{11,10},{12,13},{15,14},{16,17},{19,... | collective-permute-start | bytes 1572872 | tf_op jit(solution)/shard_map/ppermute | solution.py:276
  184.8 14.1 %collective-permute-start.37 = (bf16[512,512]{1,0:T(8,128)(2,1)S(1)}, bf16[512,512]{1,0:T(8,128)(2,1)S(1)}, u32[]{:S(2)}, u32[]{:S(2)}) collective-permute-start(bf16[512,512]{1,0:T(8,128)(2,1)S(1)} %add_convert_fusion.7), channel_id=1, source_target_pairs={{0,1},{1,2},{4,5},{5,6},{8,9},{9,10},{12,13},{13,14},{16,17},{17,1... | collective-permute-start | bytes 1572872 | tf_op jit(solution)/shard_map/ppermute | solution.py:276
  186.1 12.7 %collective-permute-start.39 = (bf16[512,512]{1,0:T(8,128)(2,1)S(1)}, bf16[512,512]{1,0:T(8,128)(2,1)S(1)}, u32[]{:S(2)}, u32[]{:S(2)}) collective-permute-start(bf16[512,512]{1,0:T(8,128)(2,1)S(1)} %add_convert_fusion.7), channel_id=1, source_target_pairs={{3,2},{2,1},{7,6},{6,5},{11,10},{10,9},{15,14},{14,13},{19,18},{18... | collective-permute-start | bytes 1572872 | tf_op jit(solution)/shard_map/ppermute | solution.py:276
  187.0 19.9 %collective-permute-start.47 = (f32[2,384,192]{1,2,0:T(8,128)S(1)}, f32[2,384,192]{1,2,0:T(8,128)S(1)}, u32[]{:S(2)}, u32[]{:S(2)}) collective-permute-start(f32[2,384,192]{1,2,0:T(8,128)S(1)} %dynamic-slice_bitcast_fusion), channel_id=1, source_target_pairs={{0,8},{4,12},{8,0},{12,4},{1,9},{5,13},{9,1},{13,5},{2,10},{6,14},... | collective-permute-start | bytes 1769480 | tf_op jit(solution)/shard_map/ppermute | solution.py:37
  194.0 16.5 %collective-permute-start.42 = (bf16[512,512]{1,0:T(8,128)(2,1)S(1)}, bf16[512,512]{1,0:T(8,128)(2,1)S(1)}, u32[]{:S(2)}, u32[]{:S(2)}) collective-permute-start(bf16[512,512]{1,0:T(8,128)(2,1)S(1)} %add_convert_fusion.3), channel_id=1, source_target_pairs={{0,1},{1,2},{4,5},{5,6},{8,9},{9,10},{12,13},{13,14},{16,17},{17,1... | collective-permute-start | bytes 1572872 | tf_op jit(solution)/shard_map/ppermute | solution.py:276
  198.2 12.3 %collective-permute-start.44 = (bf16[512,512]{1,0:T(8,128)(2,1)S(1)}, bf16[512,512]{1,0:T(8,128)(2,1)S(1)}, u32[]{:S(2)}, u32[]{:S(2)}) collective-permute-start(bf16[512,512]{1,0:T(8,128)(2,1)S(1)} %add_convert_fusion.3), channel_id=1, source_target_pairs={{3,2},{2,1},{7,6},{6,5},{11,10},{10,9},{15,14},{14,13},{19,18},{18... | collective-permute-start | bytes 1572872 | tf_op jit(solution)/shard_map/ppermute | solution.py:276
  199.2 23.0 %collective-permute-start.38 = (bf16[512,512]{1,0:T(8,128)(2,1)S(1)}, bf16[512,512]{1,0:T(8,128)(2,1)S(1)}, u32[]{:S(2)}, u32[]{:S(2)}) collective-permute-start(bf16[512,512]{1,0:T(8,128)(2,1)S(1)} %get-tuple-element.51), channel_id=1, source_target_pairs={{0,1},{1,2},{2,3},{4,5},{5,6},{6,7},{8,9},{9,10},{10,11},{12,13},{... | collective-permute-start | bytes 1572872 | tf_op jit(solution)/shard_map/ppermute | solution.py:276
  205.6 16.6 %collective-permute-start.40 = (bf16[512,512]{1,0:T(8,128)(2,1)S(1)}, bf16[512,512]{1,0:T(8,128)(2,1)S(1)}, u32[]{:S(2)}, u32[]{:S(2)}) collective-permute-start(bf16[512,512]{1,0:T(8,128)(2,1)S(1)} %get-tuple-element.52), channel_id=1, source_target_pairs={{3,2},{2,1},{1,0},{7,6},{6,5},{5,4},{11,10},{10,9},{9,8},{15,14},{... | collective-permute-start | bytes 1572872 | tf_op jit(solution)/shard_map/ppermute | solution.py:276
  207.1 15.4 %collective-permute-start.48 = (f32[1,384,192]{1,2,0:T(8,128)S(1)}, f32[1,384,192]{1,2,0:T(8,128)S(1)}, u32[]{:S(2)}, u32[]{:S(2)}) collective-permute-start(f32[1,384,192]{1,2,0:T(8,128)S(1)} %constant_dynamic-slice_fusion.2), channel_id=1, source_target_pairs={{0,4},{4,0},{8,12},{12,8},{1,5},{5,1},{9,13},{13,9},{2,6},{6,2},{1... | collective-permute-start | bytes 884744 | tf_op jit(solution)/shard_map/ppermute | solution.py:37
  211.8 21.1 %collective-permute-start.43 = (bf16[512,512]{1,0:T(8,128)(2,1)}, bf16[512,512]{1,0:T(8,128)(2,1)S(1)}, u32[]{:S(2)}, u32[]{:S(2)}) collective-permute-start(bf16[512,512]{1,0:T(8,128)(2,1)} %get-tuple-element.53), channel_id=1, source_target_pairs={{0,1},{1,2},{2,3},{4,5},{5,6},{6,7},{8,9},{9,10},{10,11},{12,13},{... | collective-permute-start | bytes 1572872 | tf_op jit(solution)/shard_map/ppermute | solution.py:276
  220.8 12.4 %collective-permute-start.45 = (bf16[512,512]{1,0:T(8,128)(2,1)}, bf16[512,512]{1,0:T(8,128)(2,1)}, u32[]{:S(2)}, u32[]{:S(2)}) collective-permute-start(bf16[512,512]{1,0:T(8,128)(2,1)} %get-tuple-element.54), channel_id=1, source_target_pairs={{3,2},{2,1},{1,0},{7,6},{6,5},{5,4},{11,10},{10,9},{9,8},{15,14},{... | collective-permute-start | bytes 1572872 | tf_op jit(solution)/shard_map/ppermute | solution.py:276
  222.6 6.8 %collective-permute-start.51 = (f32[128,192]{0,1:T(8,128)S(1)}, f32[128,192]{0,1:T(8,128)S(1)}, u32[]{:S(2)}, u32[]{:S(2)}) collective-permute-start(f32[128,192]{0,1:T(8,128)S(1)} %slice_bitcast_fusion.8), channel_id=1, source_target_pairs={{0,4},{4,0},{8,12},{12,8},{1,5},{5,1},{9,13},{13,9},{2,6},{6,2},{1... | collective-permute-start | bytes 294920 | tf_op jit(solution)/shard_map/ppermute | solution.py:37
  223.9 18.0 %collective-permute-start.49 = (f32[128,192]{0,1:T(8,128)S(1)}, f32[128,192]{0,1:T(8,128)S(1)}, u32[]{:S(2)}, u32[]{:S(2)}) collective-permute-start(f32[128,192]{0,1:T(8,128)S(1)} %bitcast.94), channel_id=1, source_target_pairs={{0,2},{1,3},{2,0},{3,1},{4,6},{5,7},{6,4},{7,5},{8,10},{9,11},{10,... | collective-permute-start | bytes 294920 | tf_op jit(solution)/shard_map/ppermute | solution.py:37
  229.5 12.5 %collective-permute-start.52 = (f32[256,192]{0,1:T(8,128)S(1)}, f32[256,192]{0,1:T(8,128)S(1)}, u32[]{:S(2)}, u32[]{:S(2)}) collective-permute-start(f32[256,192]{0,1:T(8,128)S(1)} %maximum_select_fusion.2), channel_id=1, source_target_pairs={{0,8},{4,12},{8,0},{12,4},{1,9},{5,13},{9,1},{13,5},{2,10},{6,14},... | collective-permute-start | bytes 589832 | tf_op jit(solution)/shard_map/ppermute | solution.py:37
  242.0 5.2 %collective-permute-start.53 = (f32[512,192]{0,1:T(8,128)S(1)}, f32[512,192]{0,1:T(8,128)S(1)}, u32[]{:S(2)}, u32[]{:S(2)}) collective-permute-start(f32[512,192]{0,1:T(8,128)S(1)} %maximum_select_fusion.1), channel_id=1, source_target_pairs={{0,16},{16,0},{1,17},{17,1},{2,18},{18,2},{3,19},{19,3},{4,20},{20... | collective-permute-start | bytes 1179656 | tf_op jit(solution)/shard_map/ppermute | solution.py:37
  242.1 4.5 %collective-permute-start.50 = (f32[64,192]{1,0:T(8,128)S(1)}, f32[64,192]{1,0:T(8,128)S(1)}, u32[]{:S(2)}, u32[]{:S(2)}) collective-permute-start(f32[64,192]{1,0:T(8,128)S(1)} %dynamic-slice_bitcast_fusion.1), channel_id=1, source_target_pairs={{0,1},{1,0},{2,3},{3,2},{4,5},{5,4},{6,7},{7,6},{8,9},{9,8},{10,11... | collective-permute-start | bytes 147464 | tf_op jit(solution)/shard_map/ppermute | solution.py:37
  (49 other events, 334.7 us)

commit v2 on v1

--- a/solution.py
+++ b/solution.py
@@ -10,7 +10,7 @@
 
 adapter_scaling = 0.5
 VMEM_LIMIT = 56 * 1024 * 1024
-ROW_TILE = 256
+ROW_TILE = 512
 PIECES = 4
 HALVES = 2
 QUARTER_ORDER = ((3, 2, 1, 0), (0, 3, 2, 1), (3, 0, 1, 2), (0, 1, 2, 3))
@@ -52,16 +52,20 @@
 
     def block_copies():
         copies = []
-        for number, (mask, offset) in enumerate(layout):
+        for number, group in enumerate(layout):
             block = blocks[number]
-            place = pl.multiple_of(
-                lax.bitwise_xor(position_ref[0], jnp.int32(mask)) * rows + offset, block.shape[1]
-            )
-            copies.append(
-                pltpu.make_async_copy(
-                    block, weights.at[:, pl.ds(place, block.shape[1]), :], sems.at[number]
+            size = block.shape[1]
+            for index, (mask, offset) in enumerate(group):
+                place = pl.multiple_of(
+                    lax.bitwise_xor(position_ref[0], jnp.int32(mask)) * rows + offset, size
                 )
-            )
+                copies.append(
+                    pltpu.make_async_copy(
+                        block.at[pl.ds(3 * index, 3)],
+                        weights.at[:, pl.ds(place, size), :],
+                        sems.at[len(copies)],
+                    )
+                )
         return copies
 
     def full_copies():
@@ -156,7 +160,7 @@
         out_shape=out_shape,
         scratch_shapes=[
             pltpu.VMEM((3, width, columns), jnp.bfloat16),
-            pltpu.SemaphoreType.DMA((len(blocks),)),
+            pltpu.SemaphoreType.DMA((sum(map(len, layout)),)),
             pltpu.SemaphoreType.DMA((2,)),
         ],
         input_output_aliases=aliases,
@@ -211,15 +215,93 @@
     )(quarter, gate_grad, up_grad, gate, up, low, factor)
 
 
-def gather_blocks(own):
+def move_kernel(n_in, plan, *refs):
+    ins, outs, sems = refs[:n_in], refs[n_in:-1], refs[-1]
+    copies = []
+    for number, (source, rows, target, place) in enumerate(plan):
+        block = ins[source]
+        if rows is not None:
+            block = block.at[:, pl.ds(*rows), :]
+        copies.append(
+            pltpu.make_async_copy(
+                block, outs[target].at[pl.ds(place, block.shape[0])], sems.at[number]
+            )
+        )
+    for copy in copies:
+        copy.start()
+    for copy in copies:
+        copy.wait()
+
+
+def move(arrays, shapes, plan, ahead=()):
+    anywhere = pl.BlockSpec(memory_space=pl.ANY)
+    return pl.pallas_call(
+        functools.partial(move_kernel, len(arrays) + len(ahead), plan),
+        in_specs=[anywhere] * (len(arrays) + len(ahead)),
+        out_specs=[anywhere] * len(shapes),
+        out_shape=[jax.ShapeDtypeStruct(shape, arrays[0].dtype) for shape in shapes],
+        scratch_shapes=[pltpu.SemaphoreType.DMA((len(plan),))],
+        name="move",
+    )(*arrays, *ahead)
+
+
+def nothing_kernel(*refs):
+    pass
+
+
+def hold(arrays, ahead):
+    anywhere = pl.BlockSpec(memory_space=pl.ANY)
+    return pl.pallas_call(
+        nothing_kernel,
+        in_specs=[anywhere] * (len(arrays) + len(ahead)),
+        out_specs=[anywhere] * len(arrays),
+        out_shape=[jax.ShapeDtypeStruct(array.shape, array.dtype) for array in arrays],
+        input_output_aliases={number: number for number in range(len(arrays))},
+        name="hold",
+    )(*arrays, *ahead)
+
+
+def gather_square(own, came, ahead_first, ahead_second):
+    mats, rows, columns = own.shape
+    half = rows // 2
+    near, far = came[1], came[2]
+    first, upper, lower = move(
+        [own, near, far],
+        [(3 * mats, rows, columns), (mats, half, columns), (mats, half, columns)],
+        (
+            (1, (0, half), 1, 0),
+            (2, (half, half), 2, 0),
+            (0, None, 0, 0),
+            (1, None, 0, mats),
+            (2, None, 0, 2 * mats),
+        ),
+        ahead_first,
+    )
+    upper = flip(upper, "fsdp", 2)
+    lower = flip(lower, "fsdp", 1)
+    first_other = flip(first, "cuts", 1)
+    (second,) = move(
+        [upper, lower],
+        [(2 * mats, half, columns)],
+        ((0, None, 0, 0), (1, None, 0, mats)),
+        ahead_second,
+    )
+    blocks = [first, second, first_other, flip(second, "cuts", 1)]
+    layout = [[(0, 0), (1, 0), (2, 0)], [(3, 0), (3, half)]]
+    layout += [[(mask | 4, offset) for mask, offset in group] for group in layout]
+    return blocks, tuple(map(tuple, layout)), first
+
+
+def single_flips(own):
     size = lax.axis_size("fsdp")
-    rows = own.shape[1]
-    half = rows // 2
-    whole = {0: own}
+    return {1 << n: flip(own, "fsdp", 1 << n) for n in range(size.bit_length() - 1)}
+
+
+def gather_rest(own, came):
+    size = lax.axis_size("fsdp")
+    half = own.shape[1] // 2
+    whole = {0: own, **came}
     upper, lower = {}, {}
-    bits = [1 << number for number in range(size.bit_length() - 1)]
-    for bit in bits:
-        whole[bit] = flip(own, "fsdp", bit)
     for mask, block in whole.items():
         upper[mask], lower[mask] = block[:, :half], block[:, half:]
     for mask in range(size):
@@ -230,17 +312,14 @@
         if mask not in whole:
             low = mask & -mask
             lower[mask] = flip(lower[mask ^ low], "fsdp", low)
-    blocks, layout = [], []
-    for mask in range(size):
-        if mask in whole:
-            blocks.append(whole[mask])
-            layout.append((mask, 0))
-        else:
-            blocks += [upper[mask], lower[mask]]
-            layout += [(mask, 0), (mask, half)]
-    other = [flip(block, "cuts", 1) for block in blocks]
-    layout = layout + [(mask | size, offset) for mask, offset in layout]
-    return blocks + other, tuple(layout)
+    first = jnp.concatenate(list(whole.values()))
+    rest = [mask for mask in range(size) if mask not in whole]
+    second = jnp.concatenate([part[mask] for mask in rest for part in (upper, lower)])
+    layout = [[(mask, 0) for mask in whole]]
+    layout.append([(mask, offset) for mask in rest for offset in (0, half)])
+    blocks = [first, second, flip(first, "cuts", 1), flip(second, "cuts", 1)]
+    layout += [[(mask | size, offset) for mask, offset in group] for group in layout]
+    return blocks, tuple(map(tuple, layout))
 
 
 def sum_over_plane(parts, cut, place):
@@ -269,23 +348,6 @@
         bit *= 2
     other = flip(rows, "cuts", 1)
     return jnp.where(cut == 0, jnp.concatenate([rows, other]), jnp.concatenate([other, rows]))
-
-
-def sum_over_line(slots, place):
-    first, second, third, last = slots
-    shift = lambda array, pairs: lax.ppermute(array, "tp", pairs)
-    plus = lambda a, b: (a.astype(jnp.float32) + b.astype(jnp.float32)).astype(jnp.bfloat16)
-    came = shift(first, [(0, 1), (3, 2)])
-    onward = plus(second, came)
-    from_left = shift(onward, [(0, 1), (1, 2)])
-    from_right = shift(onward, [(3, 2), (2, 1)])
-    to_right = plus(jnp.where(place == 2, first, third), from_left)
-    to_left = plus(jnp.where(place == 1, first, third), from_right)
-    from_left = shift(to_right, [(0, 1), (1, 2), (2, 3)])
-    from_right = shift(to_left, [(3, 2), (2, 1), (1, 0)])
-    return (last + from_left.astype(jnp.float32) + from_right.astype(jnp.float32)).astype(
-        jnp.bfloat16
-    )
 
 
 def per_device(
@@ -312,8 +374,15 @@
     gradient_scaling = adapter_scaling / math.sqrt(rows * groups)
     position = lax.axis_index(("cuts", "fsdp")).astype(jnp.int32).reshape(1)
 
+    lows = [
+        matrix_product(tokens, gate_adapter_input_factor).astype(jnp.bfloat16),
+        matrix_product(tokens, up_adapter_input_factor).astype(jnp.bfloat16),
+        matrix_product(cotangent, down_leave).astype(jnp.bfloat16),
+    ]
+    factors = [gate_adapter_output_factor, up_adapter_output_factor, down_adapter_input_factor]
     columns = hidden_size // PIECES
-    gathered = []
+    state = ()
+    came, states, firsts = [], [], []
     for piece in range(PIECES):
         span = slice(piece * columns, (piece + 1) * columns)
         own = jnp.stack(
@@ -323,44 +392,76 @@
                 down_frozen_matrix[span].T,
             ]
         )
-        gathered.append(gather_blocks(own))
-
-    lows = [
-        matrix_product(tokens, gate_adapter_input_factor).astype(jnp.bfloat16),
-        matrix_product(tokens, up_adapter_input_factor).astype(jnp.bfloat16),
-        matrix_product(cotangent, down_leave).astype(jnp.bfloat16),
-    ]
-    factors = [gate_adapter_output_factor, up_adapter_output_factor, down_adapter_input_factor]
-    state = ()
-    for piece in range(PIECES):
-        blocks, layout = gathered[piece]
+        square = lax.axis_size("fsdp") == 4
+        if square and piece == 2:
+            (own,) = hold([own], [firsts[0]])
+        if square and piece > 2:
+            (own,) = hold([own], [states[piece - 3][-1]])
+        came.append(single_flips(own))
+        if square:
+            blocks, layout, first = gather_square(
+                own,
+                came[piece],
+                [states[piece - 2][-1]] if piece >= 2 else [],
+                [states[piece - 1][-1]] if piece >= 1 else [],
+            )
+            firsts.append(first)
+        else:
+            blocks, layout = gather_rest(own, came[piece])
         state = forward_piece(
             piece, columns, position, tokens, cotangent, lows, factors, blocks, layout, state
         )
+        states.append(state)
     hidden, gate_grad, up_grad, gate_full, up_full, low = state
 
     input_factor = jnp.concatenate([gate_adapter_input_factor, up_adapter_input_factor], axis=1)
     order = jnp.asarray(QUARTER_ORDER, jnp.int32)[quarter]
-    results = []
-    for half in range(HALVES):
-        slots = [
-            token_grad(
-                order[k : k + 1],
-                half,
-                jnp.float32 if k == quarters - 1 else jnp.bfloat16,
-                gate_grad,
-                up_grad,
-                gate_full,
-                up_full,
-                low,
-                input_factor,
-                width // quarters,
-            )
-            for k in range(quarters)
+    share = lambda k, half: token_grad(
+        order[k : k + 1],
+        half,
+        jnp.float32 if k == quarters - 1 else jnp.bfloat16,
+        gate_grad,
+        up_grad,
+        gate_full,
+        up_full,
+        low,
+        input_factor,
+        width // quarters,
+    )
+    shift = lambda array, pairs: lax.ppermute(array, "tp", pairs)
+    plus = lambda a, b: (a.astype(jnp.float32) + b.astype(jnp.float32)).astype(jnp.bfloat16)
+    first = [share(0, half) for half in range(HALVES)]
+    came = [shift(part, [(0, 1), (3, 2)]) for part in first]
+    second = [share(1, half) for half in range(HALVES)]
+    sums = [plus(second[half], came[half]) for half in range(HALVES)]
+    from_left = [shift(part, [(0, 1), (1, 2)]) for part in sums]
+    from_right = [shift(part, [(3, 2), (2, 1)]) for part in sums]
+    gate_grad, up_grad, hidden = hold([gate_grad, up_grad, hidden], sums)
+    third = [share(2, half) for half in range(HALVES)]
+    last = [share(3, half) for half in range(HALVES)]
+    hidden, gate_grad, up_grad = hold(
+        [hidden, gate_grad, up_grad], third + last + [from_left[0], from_right[0]]
+    )
+    to_right = [
+        plus(jnp.where(quarter == 2, first[half], third[half]), from_left[half])
+        for half in range(HALVES)
+    ]
+    to_left = [
+        plus(jnp.where(quarter == 1, first[half], third[half]), from_right[half])
+        for half in range(HALVES)
+    ]
+    from_left = [shift(part, [(0, 1), (1, 2), (2, 3)]) for part in to_right]
+    from_right = [shift(part, [(3, 2), (2, 1), (1, 0)]) for part in to_left]
+    token_input_gradient = jnp.concatenate(
+        [
+            (
+                last[half]
+                + from_left[half].astype(jnp.float32)
+                + from_right[half].astype(jnp.float32)
+            ).astype(jnp.bfloat16)
+            for half in range(HALVES)
         ]
-        results.append(sum_over_line(slots, quarter))
-    token_input_gradient = jnp.concatenate(results)
-
+    )
     down_low = matrix_product(hidden, down_adapter_input_factor).astype(jnp.bfloat16)
     narrow = gradient_scaling * jnp.concatenate(
         [

time: 250 us -> 489 us (1.96)
  Pallas kernels: 85.4 us -> 333 us
  waiting for transfers between devices: 43.8 us -> 33.5 us
  starting transfers between devices: 65.7 us -> 58.2 us
  other arithmetic: 10 us -> 16.9 us
    pallas_call x0 -> x12, Pallas kernels: none -> 247 us  [the longest x8 247 us: move(): pl.pallas_call(functools.partial(move_kernel, len(arrays) + len(ahead), p...]
    ppermute x44 -> x32, waiting for transfers between devices: 38.5 us -> 24.5 us  [flip(): return lax.ppermute(array, axis, [(i, i ^ bit) for i in range(size)])]
    ppermute x44 -> x32, starting transfers between devices: 35.9 us -> 30.1 us  [flip(): return lax.ppermute(array, axis, [(i, i ^ bit) for i in range(size)])]
    unnamed x125 -> x97, local copies, waits for them, and re-layouts: 9.94 us -> 12.9 us
  transfers between devices with their start and end apart: 54 -> 42, of which waited for: 14 -> 10; matrix products, arithmetic and copies ran while one was open for 10% -> 7% of each run, Pallas kernels for 30% -> 64%
where the time goes in v2:
time: 489 us; the launch traced here: 488 us
  Pallas kernels  333 us (68%)
  starting transfers between devices  58.2 us (12%)
  waiting for transfers between devices  33.5 us (7%)
  local copies, waits for them, and re-layouts  22.4 us (5%)
  matrix products  22.3 us (5%)
  other arithmetic  16.9 us (3%)
    pallas_call x8, Pallas kernels, move(): pl.pallas_call(functools.partial(move_kernel, len(arrays) + len(ahead), p...  247 us
    pallas_call x4, Pallas kernels, forward_piece(): pl.pallas_call(functools.partial(forward_kernel, len(before), layout, pie...  44.4 us
    pallas_call x8, Pallas kernels, token_grad(): pl.pallas_call(token_grad_kernel, grid_spec=pltpu.PrefetchScalarGridSpec(...  41.6 us
    ppermute x32, starting transfers between devices, flip(): return lax.ppermute(array, axis, [(i, i ^ bit) for i in range(size)])  30.1 us
    ppermute x10, starting transfers between devices, per_device(): shift = lambda array, pairs: lax.ppermute(array, 'tp', pairs)  28.1 us
    ppermute x32, waiting for transfers between devices, flip(): return lax.ppermute(array, axis, [(i, i ^ bit) for i in range(size)])  24.5 us
    unnamed x97, local copies, waits for them, and re-layouts  12.9 us
    dot_general x3, matrix products, matrix_product(): return jnp.dot(left, right, preferred_element_type=jnp.float32)  12.4 us
  transfers between devices with their start and end apart: 42, of which 10 were waited for; matrix products, arithmetic and copies ran while one was open for 7% of the time, Pallas kernels for 64%

profile of v2, /device:TPU:0, one launch (start us, length us, event | category | flops | bytes accessed | tf_op | source)
XLA Modules:
  0.0 488.2 jit_solution(14024058131279787892)
XLA Ops:
  0.6 1.2 fusion.12
  1.9 1.4 slice_bitcast_fusion
  3.4 3.0 collective-permute-start
  6.4 1.5 collective-permute-start.1
  8.7 7.6 %collective-permute-done.refs_1_ = bf16[3,256,256]{2,1,0:T(8,128)(2,1)S(1)} collective-permute-done((bf16[3,256,256]{2,1,0:T(8,128)(2,1)S(1)}, bf16[3,256,256]{2,1,0:T(8,128)(2,1)S(1)}, u32[]{:S(2)}, u32[]{:S(2)}) %collective-permute-start) | collective-permute-done | bytes 393248 | tf_op jit(solution)/shard_map/ppermute | solution.py:37
  16.3 2.1 collective-permute-done.1.refs_2_
  19.2 48.8 %move.8 = (bf16[9,256,256]{2,1,0:T(8,128)(2,1)}, bf16[3,128,256]{2,1,0:T(8,128)(2,1)}, bf16[3,128,256]{2,1,0:T(8,128)(2,1)}) custom-call(bf16[3,256,256]{2,1,0:T(8,128)(2,1)} %copy-done.22, bf16[3,256,256]{2,1,0:T(8,128)(2,1)} %copy-done.31, bf16[3,256,256]{2,1,0:T(8,128)(2,1)} %copy-done.32), custom_call_target="tpu_custom_call" | custom-call | tf_op jit(solution)/shard_map/move/pallas_call | solution.py:238
  68.1 4.1 fusion.14.refs_2_
  72.3 1.6 collective-permute-start.2
  74.6 4.1 fusion.15.refs_3_
  79.5 48.8 %move.10 = (bf16[9,256,256]{2,1,0:T(8,128)(2,1)}, bf16[3,128,256]{2,1,0:T(8,128)(2,1)}, bf16[3,128,256]{2,1,0:T(8,128)(2,1)}) custom-call(bf16[3,256,256]{2,1,0:T(8,128)(2,1)} %copy-done.21, bf16[3,256,256]{2,1,0:T(8,128)(2,1)} %copy-done.30, bf16[3,256,256]{2,1,0:T(8,128)(2,1)} %collective-permute-done.9.refs_2_), custom_call_target="tpu_custom_call" | custom-call | tf_op jit(solution)/shard_map/move/pallas_call | solution.py:238
  128.4 13.0 %move.9.refs_9_ = bf16[6,128,256]{2,1,0:T(8,128)(2,1)} custom-call(bf16[3,128,256]{2,1,0:T(8,128)(2,1)} %collective-permute-done.2.refs_0_, bf16[3,128,256]{2,1,0:T(8,128)(2,1)} %collective-permute-done.3.refs_1_), custom_call_target="tpu_custom_call" | custom-call | tf_op jit(solution)/shard_map/move/pallas_call | solution.py:238
  142.8 1.3 collective-permute-start.16
  144.6 4.1 fusion.16.refs_4_
  149.6 1.5 collective-permute-start.10
  152.2 11.1 %forward_piece.4 = (bf16[1024,1024]{1,0:T(8,128)(2,1)}, bf16[1024,1024]{1,0:T(8,128)(2,1)}, bf16[1024,1024]{1,0:T(8,128)(2,1)}, bf16[2048,1024]{1,0:T(8,128)(2,1...) custom-call(s32[1]{0:T(128)} %bitcast.1.position_ref, bf16[1024,2048]{1,0:T(8,128)(2,1)} %refs_0_.7, ...), custom_call_target="tpu_custom_call" | custom-call | flops 3221225472 | bytes 15204352 | tf_op jit(solution)/shard_map/forward_piece/pallas_call | solution.py:155
  164.0 48.8 %move.13 = (bf16[9,256,256]{2,1,0:T(8,128)(2,1)}, bf16[3,128,256]{2,1,0:T(8,128)(2,1)}, bf16[3,128,256]{2,1,0:T(8,128)(2,1)}) custom-call(bf16[3,256,256]{2,1,0:T(8,128)(2,1)} %hold.5.refs_0_, bf16[3,256,256]{2,1,0:T(8,128)(2,1)} %copy-done.33, bf16[3,256,256]{2,1,0:T(8,128)(2,1)} %collective-permute-done.17.refs_2_, ...), custom_call_target="tpu_custom_call" | custom-call | tf_op jit(solution)/shard_map/move/pallas_call | solution.py:238
  213.6 13.0 %move.11.refs_9_ = bf16[6,128,256]{2,1,0:T(8,128)(2,1)} custom-call(bf16[3,128,256]{2,1,0:T(8,128)(2,1)} %copy-done.42, bf16[3,128,256]{2,1,0:T(8,128)(2,1)} %collective-permute-done.11.refs_1_, f32[1024,128]{1,0:T(8,128)} %get-tuple-element.48.refs_1_.refs_2_.refs_17_.refs_3_), custom_call_target="tpu_custom_call" | custom-call | tf_op jit(solution)/shard_map/move/pallas_call | solution.py:238
  229.6 1.5 collective-permute-start.18
  232.1 11.1 %forward_piece.5 = (bf16[1024,1024]{1,0:T(8,128)(2,1)}, bf16[1024,1024]{1,0:T(8,128)(2,1)}, bf16[1024,1024]{1,0:T(8,128)(2,1)}, bf16[2048,1024]{1,0:T(8,128)(2,1...) custom-call(s32[1]{0:T(128)} %bitcast.1.position_ref, ...), custom_call_target="tpu_custom_call", output_to_operand_aliasing={{0}: (13, {}), {1}: (14, {}), {2}: (15, {}), {3}: (16, {}),... | custom-call | flops 3221225472 | bytes 15204352 | tf_op jit(solution)/shard_map/forward_piece/pallas_call | solution.py:155
  244.2 48.8 %move.12 = (bf16[9,256,256]{2,1,0:T(8,128)(2,1)}, bf16[3,128,256]{2,1,0:T(8,128)(2,1)}, bf16[3,128,256]{2,1,0:T(8,128)(2,1)}) custom-call(bf16[3,256,256]{2,1,0:T(8,128)(2,1)} %hold.4.refs_0_, bf16[3,256,256]{2,1,0:T(8,128)(2,1)} %copy-done.34, bf16[3,256,256]{2,1,0:T(8,128)(2,1)} %copy-done.35, f32[1024,128]{1,0:T(8,128)} %get-tuple-element.57.refs_3_.refs_2_.refs_17_), custom_call_target="tpu_custom_call" | custom-call | tf_op jit(solution)/shard_map/move/pallas_call | solution.py:238
  293.7 13.0 %move.14.refs_9_ = bf16[6,128,256]{2,1,0:T(8,128)(2,1)} custom-call(bf16[3,128,256]{2,1,0:T(8,128)(2,1)} %copy-done.41, bf16[3,128,256]{2,1,0:T(8,128)(2,1)} %collective-permute-done.19.refs_1_, f32[1024,128]{1,0:T(8,128)} %get-tuple-element.57.refs_3_.refs_2_.refs_17_), custom_call_target="tpu_custom_call" | custom-call | tf_op jit(solution)/shard_map/move/pallas_call | solution.py:238
  307.8 1.1 collective-permute-start.15
  310.1 11.1 %forward_piece.6 = (bf16[1024,1024]{1,0:T(8,128)(2,1)}, bf16[1024,1024]{1,0:T(8,128)(2,1)}, bf16[1024,1024]{1,0:T(8,128)(2,1)}, bf16[2048,1024]{1,0:T(8,128)(2,1...) custom-call(s32[1]{0:T(128)} %bitcast.1.position_ref, ...), custom_call_target="tpu_custom_call", output_to_operand_aliasing={{0}: (13, {}), {1}: (14, {}), {2}: (15, {}), {3}: (16, {}),... | custom-call | flops 3221225472 | bytes 15204352 | tf_op jit(solution)/shard_map/forward_piece/pallas_call | solution.py:155
  321.9 13.0 %move.15.refs_9_ = bf16[6,128,256]{2,1,0:T(8,128)(2,1)} custom-call(bf16[3,128,256]{2,1,0:T(8,128)(2,1)} %copy-done.43, bf16[3,128,256]{2,1,0:T(8,128)(2,1)} %copy-done.44, f32[1024,128]{1,0:T(8,128)} %get-tuple-element.69.refs_2_.refs_17_), custom_call_target="tpu_custom_call" | custom-call | tf_op jit(solution)/shard_map/move/pallas_call | solution.py:238
  337.3 1.1 pad_maximum_fusion.1.factor_ref
  339.2 11.1 %forward_piece.7 = (bf16[1024,1024]{1,0:T(8,128)(2,1)}, bf16[1024,1024]{1,0:T(8,128)(2,1)}, bf16[1024,1024]{1,0:T(8,128)(2,1)}, bf16[2048,1024]{1,0:T(8,128)(2,1...) custom-call(s32[1]{0:T(128)} %bitcast.1.position_ref, ...), custom_call_target="tpu_custom_call", output_to_operand_aliasing={{0}: (13, {}), {1}: (14, {}), {2}: (15, {}), {3}: (16, {}),... | custom-call | flops 3221225472 | bytes 15204352 | tf_op jit(solution)/shard_map/forward_piece/pallas_call | solution.py:155
  350.3 5.1 %token_grad.9 = bf16[512,512]{1,0:T(8,128)(2,1)} custom-call(s32[1]{0:T(128)} %bitcast.19.quarter_ref, bf16[1024,1024]{1,0:T(8,128)(2,1)} %get-tuple-element.75.gate_grad_ref.refs_0_, bf16[1024,1024]{1,0:T(8,128)(2,1)} %get-tuple-element.76.up_grad_ref.refs_1_, bf16[2048,1024]{1,0:T(8,128)(2,1)} %get-tuple-element.78.gate_ref, ...), custom_call_target="tpu_custom_call" | custom-call | flops 1073741824 | bytes 4718592 | tf_op jit(solution)/shard_map/token_grad/pallas_call | solution.py:192
  355.4 5.6 %token_grad.11 = bf16[512,512]{1,0:T(8,128)(2,1)} custom-call(s32[1]{0:T(128)} %bitcast.19.quarter_ref, bf16[1024,1024]{1,0:T(8,128)(2,1)} %get-tuple-element.75.gate_grad_ref.refs_0_, bf16[1024,1024]{1,0:T(8,128)(2,1)} %get-tuple-element.76.up_grad_ref.refs_1_, bf16[2048,1024]{1,0:T(8,128)(2,1)} %get-tuple-element.78.gate_ref, ...), custom_call_target="tpu_custom_call" | custom-call | flops 1073741824 | bytes 4718592 | tf_op jit(solution)/shard_map/token_grad/pallas_call | solution.py:192
  361.0 4.3 collective-permute-start.24
  365.3 1.3 collective-permute-start.25
  368.1 1.3 copy.87
  369.4 5.0 %token_grad.8 = bf16[512,512]{1,0:T(8,128)(2,1)} custom-call(s32[1]{0:T(128)} %bitcast.18.quarter_ref, bf16[1024,1024]{1,0:T(8,128)(2,1)} %get-tuple-element.75.gate_grad_ref.refs_0_, bf16[1024,1024]{1,0:T(8,128)(2,1)} %get-tuple-element.76.up_grad_ref.refs_1_, bf16[2048,1024]{1,0:T(8,128)(2,1)} %get-tuple-element.78.gate_ref, ...), custom_call_target="tpu_custom_call" | custom-call | flops 1073741824 | bytes 4718592 | tf_op jit(solution)/shard_map/token_grad/pallas_call | solution.py:192
  374.4 5.1 %token_grad.10 = bf16[512,512]{1,0:T(8,128)(2,1)} custom-call(s32[1]{0:T(128)} %bitcast.18.quarter_ref, bf16[1024,1024]{1,0:T(8,128)(2,1)} %get-tuple-element.75.gate_grad_ref.refs_0_, bf16[1024,1024]{1,0:T(8,128)(2,1)} %get-tuple-element.76.up_grad_ref.refs_1_, bf16[2048,1024]{1,0:T(8,128)(2,1)} %get-tuple-element.78.gate_ref, ...), custom_call_target="tpu_custom_call" | custom-call | flops 1073741824 | bytes 4718592 | tf_op jit(solution)/shard_map/token_grad/pallas_call | solution.py:192
  379.5 1.2 add_convert_fusion.7.refs_3_
  380.7 1.8 collective-permute-start.26
  383.4 4.7 collective-permute-done.25
  388.1 2.0 add_convert_fusion.6.refs_4_
  390.1 5.3 %token_grad.12.refs_5_ = f32[512,512]{1,0:T(8,128)} custom-call(s32[1]{0:T(128)} %bitcast.quarter_ref, bf16[1024,1024]{1,0:T(8,128)(2,1)} %get-tuple-element.81.gate_grad_ref.refs_1_, bf16[1024,1024]{1,0:T(8,128)(2,1)} %get-tuple-element.82.up_grad_ref.refs_2_, bf16[2048,1024]{1,0:T(8,128)(2,1)} %get-tuple-element.78.gate_ref, ...), custom_call_target="tpu_custom_call" | custom-call | flops 1073741824 | bytes 4718592 | tf_op jit(solution)/shard_map/token_grad/pallas_call | solution.py:192
  395.4 5.3 %token_grad.14.refs_6_ = f32[512,512]{1,0:T(8,128)} custom-call(s32[1]{0:T(128)} %bitcast.quarter_ref, bf16[1024,1024]{1,0:T(8,128)(2,1)} %get-tuple-element.81.gate_grad_ref.refs_1_, bf16[1024,1024]{1,0:T(8,128)(2,1)} %get-tuple-element.82.up_grad_ref.refs_2_, bf16[2048,1024]{1,0:T(8,128)(2,1)} %get-tuple-element.78.gate_ref, ...), custom_call_target="tpu_custom_call" | custom-call | flops 1073741824 | bytes 4718592 | tf_op jit(solution)/shard_map/token_grad/pallas_call | solution.py:192
  400.6 5.1 %token_grad.13.refs_3_ = bf16[512,512]{1,0:T(8,128)(2,1)} custom-call(s32[1]{0:T(128)} %bitcast.20.quarter_ref, bf16[1024,1024]{1,0:T(8,128)(2,1)} %get-tuple-element.81.gate_grad_ref.refs_1_, bf16[1024,1024]{1,0:T(8,128)(2,1)} %get-tuple-element.82.up_grad_ref.refs_2_, bf16[2048,1024]{1,0:T(8,128)(2,1)} %get-tuple-element.78.gate_ref, ...), custom_call_target="tpu_custom_call" | custom-call | flops 1073741824 | bytes 4718592 | tf_op jit(solution)/shard_map/token_grad/pallas_call | solution.py:192
  405.7 5.1 %token_grad.15.refs_4_ = bf16[512,512]{1,0:T(8,128)(2,1)} custom-call(s32[1]{0:T(128)} %bitcast.20.quarter_ref, bf16[1024,1024]{1,0:T(8,128)(2,1)} %get-tuple-element.81.gate_grad_ref.refs_1_, bf16[1024,1024]{1,0:T(8,128)(2,1)} %get-tuple-element.82.up_grad_ref.refs_2_, bf16[2048,1024]{1,0:T(8,128)(2,1)} %get-tuple-element.78.gate_ref, ...), custom_call_target="tpu_custom_call" | custom-call | flops 1073741824 | bytes 4718592 | tf_op jit(solution)/shard_map/token_grad/pallas_call | solution.py:192
  412.8 2.1 fusion.17
  414.9 4.5 convolution_bitcast_fusion.1
  421.7 2.1 fusion.18
  426.2 1.1 fusion.7
  427.3 3.2 collective-permute-done.34
  430.5 1.4 fusion.10
  433.0 1.2 collective-permute-start.35
  434.2 4.4 collective-permute-start.30
  439.3 1.7 add_convert_fusion.5
  441.0 4.1 collective-permute-start.27
  445.1 1.3 collective-permute-start.29
  446.4 2.1 collective-permute-done.35
  448.5 1.1 bitcast_add_fusion
  449.7 1.2 collective-permute-start.36
  451.2 1.3 add_convert_fusion.2
  452.5 7.8 %collective-permute-start.31 = (bf16[512,512]{1,0:T(8,128)(2,1)}, bf16[512,512]{1,0:T(8,128)(2,1)S(1)}, u32[]{:S(2)}, u32[]{:S(2)}) collective-permute-start(bf16[512,512]{1,0:T(8,128)(2,1)} %get-tuple-element.89), channel_id=1, source_target_pairs={{0,1},{1,2},{2,3},{4,5},{5,6},{6,7},{8,9},{9,10},{10,11},{12,13},{... | collective-permute-start | bytes 1572872 | tf_op jit(solution)/shard_map/ppermute | solution.py:431
  460.4 1.4 collective-permute-start.33
  464.0 5.1 %collective-permute-start.37 = (f32[128,192]{0,1:T(8,128)S(1)}, f32[128,192]{0,1:T(8,128)S(1)}, u32[]{:S(2)}, u32[]{:S(2)}) collective-permute-start(f32[128,192]{0,1:T(8,128)S(1)} %bitcast.94), channel_id=1, source_target_pairs={{0,2},{1,3},{2,0},{3,1},{4,6},{5,7},{6,4},{7,5},{8,10},{9,11},{10,... | collective-permute-start | bytes 294920 | tf_op jit(solution)/shard_map/ppermute | solution.py:37
  470.1 3.5 collective-permute-done.31
  473.6 1.3 add_convert_fusion
  474.9 6.9 %collective-permute-done.37 = f32[128,192]{0,1:T(8,128)S(1)} collective-permute-done((f32[128,192]{0,1:T(8,128)S(1)}, f32[128,192]{0,1:T(8,128)S(1)}, u32[]{:S(2)}, u32[]{:S(2)}) %collective-permute-start.37) | collective-permute-done | bytes 98336 | tf_op jit(solution)/shard_map/ppermute | solution.py:37
  484.1 2.5 collective-permute-done.38
  (194 shorter events, 38.4 us)
Async XLA Ops:
  0.6 144.0 %copy-start = (bf16[2048,64]{0,1:T(8,128)(2,1)S(1)}, bf16[2048,64]{0,1:T(8,128)(2,1)}, u32[]{:S(2)}) copy-start(bf16[2048,64]{0,1:T(8,128)(2,1)} %param.22) | copy-start | bytes 786436
  3.4 15.1 %copy-start.22 = (bf16[3,256,256]{2,1,0:T(8,128)(2,1)}, bf16[3,256,256]{2,1,0:T(8,128)(2,1)S(1)}, u32[]{:S(2)}) copy-start(bf16[3,256,256]{2,1,0:T(8,128)(2,1)S(1)} %pad_maximum_fusion.3.refs_0_) | copy-start | bytes 1179652
  3.4 12.9 %collective-permute-start = (bf16[3,256,256]{2,1,0:T(8,128)(2,1)S(1)}, bf16[3,256,256]{2,1,0:T(8,128)(2,1)S(1)}, u32[]{:S(2)}, u32[]{:S(2)}) collective-permute-start(bf16[3,256,256]{2,1,0:T(8,128)(2,1)S(1)} %pad_maximum_fusion.3.refs_0_), channel_id=1, source_target_pairs={{0,4},{4,0},{8,12},{12,8},{1,5},{5,1},{9,13},{13,9},{2,6},{6,2},{1... | collective-permute-start | bytes 1179656 | tf_op jit(solution)/shard_map/ppermute | solution.py:37
  6.4 12.0 %collective-permute-start.1 = (bf16[3,256,256]{2,1,0:T(8,128)(2,1)S(1)}, bf16[3,256,256]{2,1,0:T(8,128)(2,1)S(1)}, u32[]{:S(2)}, u32[]{:S(2)}) collective-permute-start(bf16[3,256,256]{2,1,0:T(8,128)(2,1)S(1)} %pad_maximum_fusion.3.refs_0_), channel_id=1, source_target_pairs={{0,8},{4,12},{8,0},{12,4},{1,9},{5,13},{9,1},{13,5},{2,10},{6,14},... | collective-permute-start | bytes 1179656 | tf_op jit(solution)/shard_map/ppermute | solution.py:37
  8.1 64.2 %copy-start.21 = (bf16[3,256,256]{2,1,0:T(8,128)(2,1)}, bf16[3,256,256]{2,1,0:T(8,128)(2,1)S(1)}, u32[]{:S(2)}) copy-start(bf16[3,256,256]{2,1,0:T(8,128)(2,1)S(1)} %pad_maximum_fusion.4.refs_0_) | copy-start | bytes 1179652
  8.1 70.7 %collective-permute-start.8 = (bf16[3,256,256]{2,1,0:T(8,128)(2,1)S(1)}, bf16[3,256,256]{2,1,0:T(8,128)(2,1)S(1)}, u32[]{:S(2)}, u32[]{:S(2)}) collective-permute-start(bf16[3,256,256]{2,1,0:T(8,128)(2,1)S(1)} %pad_maximum_fusion.4.refs_0_), channel_id=1, source_target_pairs={{0,4},{4,0},{8,12},{12,8},{1,5},{5,1},{9,13},{13,9},{2,6},{6,2},{1... | collective-permute-start | bytes 1179656 | tf_op jit(solution)/shard_map/ppermute | solution.py:37
  8.7 70.1 %collective-permute-start.9 = (bf16[3,256,256]{2,1,0:T(8,128)(2,1)S(1)}, bf16[3,256,256]{2,1,0:T(8,128)(2,1)}, u32[]{:S(2)}, u32[]{:S(2)}) collective-permute-start(bf16[3,256,256]{2,1,0:T(8,128)(2,1)S(1)} %pad_maximum_fusion.4.refs_0_), channel_id=1, source_target_pairs={{0,8},{4,12},{8,0},{12,4},{1,9},{5,13},{9,1},{13,5},{2,10},{6,14},... | collective-permute-start | bytes 1179656 | tf_op jit(solution)/shard_map/ppermute | solution.py:37
  68.0 6.6 %copy-start.39 = (bf16[2048,64]{0,1:T(8,128)(2,1)S(1)}, bf16[2048,64]{0,1:T(8,128)(2,1)}, u32[]{:S(2)}) copy-start(bf16[2048,64]{0,1:T(8,128)(2,1)} %param.18) | copy-start | bytes 786436
  68.0 83.1 %collective-permute-start.4 = (bf16[9,256,256]{2,1,0:T(8,128)(2,1)}, bf16[9,256,256]{2,1,0:T(8,128)(2,1)S(1)}, u32[]{:S(2)}, u32[]{:S(2)}) collective-permute-start(bf16[9,256,256]{2,1,0:T(8,128)(2,1)} %get-tuple-element.45.refs_8_.refs_1_), channel_id=1, source_target_pairs={{0,16},{16,0},{1,17},{17,1},{2,18},{18,2},{3,19},{19,3},{4,20},{20... | collective-permute-start | bytes 3538952 | tf_op jit(solution)/shard_map/ppermute | solution.py:37
  72.3 56.1 %collective-permute-start.2 = (bf16[3,128,256]{2,1,0:T(8,128)(2,1)}, bf16[3,128,256]{2,1,0:T(8,128)(2,1)}, u32[]{:S(2)}, u32[]{:S(2)}) collective-permute-start(bf16[3,128,256]{2,1,0:T(8,128)(2,1)} %get-tuple-element.46), channel_id=1, source_target_pairs={{0,8},{4,12},{8,0},{12,4},{1,9},{5,13},{9,1},{13,5},{2,10},{6,14},... | collective-permute-start | bytes 589832 | tf_op jit(solution)/shard_map/ppermute | solution.py:37
  73.9 54.5 %collective-permute-start.3 = (bf16[3,128,256]{2,1,0:T(8,128)(2,1)}, bf16[3,128,256]{2,1,0:T(8,128)(2,1)}, u32[]{:S(2)}, u32[]{:S(2)}) collective-permute-start(bf16[3,128,256]{2,1,0:T(8,128)(2,1)} %get-tuple-element.47), channel_id=1, source_target_pairs={{0,4},{4,0},{8,12},{12,8},{1,5},{5,1},{9,13},{13,9},{2,6},{6,2},{1... | collective-permute-start | bytes 589832 | tf_op jit(solution)/shard_map/ppermute | solution.py:37
  128.3 101.3 %collective-permute-start.12 = (bf16[9,256,256]{2,1,0:T(8,128)(2,1)}, bf16[9,256,256]{2,1,0:T(8,128)(2,1)S(1)}, u32[]{:S(2)}, u32[]{:S(2)}) collective-permute-start(bf16[9,256,256]{2,1,0:T(8,128)(2,1)} %get-tuple-element.49.refs_8_), channel_id=1, source_target_pairs={{0,16},{16,0},{1,17},{17,1},{2,18},{18,2},{3,19},{19,3},{4,20},{20... | collective-permute-start | bytes 3538952 | tf_op jit(solution)/shard_map/ppermute | solution.py:37
  141.4 8.1 %collective-permute-start.5 = (bf16[6,128,256]{2,1,0:T(8,128)(2,1)}, bf16[6,128,256]{2,1,0:T(8,128)(2,1)}, u32[]{:S(2)}, u32[]{:S(2)}) collective-permute-start(bf16[6,128,256]{2,1,0:T(8,128)(2,1)} %move.9.refs_9_), channel_id=1, source_target_pairs={{0,16},{16,0},{1,17},{17,1},{2,18},{18,2},{3,19},{19,3},{4,20},{20... | collective-permute-start | bytes 1179656 | tf_op jit(solution)/shard_map/ppermute | solution.py:37
  142.8 6.0 %copy-start.29 = (bf16[1024,64]{0,1:T(8,128)(2,1)S(1)}, bf16[1024,64]{0,1:T(8,128)(2,1)}, u32[]{:S(2)}) copy-start(bf16[1024,64]{0,1:T(8,128)(2,1)} %param.21) | copy-start | bytes 393220
  142.8 20.5 %collective-permute-start.16 = (bf16[3,256,256]{2,1,0:T(8,128)(2,1)}, bf16[3,256,256]{2,1,0:T(8,128)(2,1)S(1)}, u32[]{:S(2)}, u32[]{:S(2)}) collective-permute-start(bf16[3,256,256]{2,1,0:T(8,128)(2,1)} %hold.5.refs_0_), channel_id=1, source_target_pairs={{0,4},{4,0},{8,12},{12,8},{1,5},{5,1},{9,13},{13,9},{2,6},{6,2},{1... | collective-permute-start | bytes 1179656 | tf_op jit(solution)/shard_map/ppermute | solution.py:37
  144.1 19.1 %collective-permute-start.17 = (bf16[3,256,256]{2,1,0:T(8,128)(2,1)}, bf16[3,256,256]{2,1,0:T(8,128)(2,1)}, u32[]{:S(2)}, u32[]{:S(2)}) collective-permute-start(bf16[3,256,256]{2,1,0:T(8,128)(2,1)} %hold.5.refs_0_), channel_id=1, source_target_pairs={{0,8},{4,12},{8,0},{12,4},{1,9},{5,13},{9,1},{13,5},{2,10},{6,14},... | collective-permute-start | bytes 1179656 | tf_op jit(solution)/shard_map/ppermute | solution.py:37
  149.6 63.3 %collective-permute-start.10 = (bf16[3,128,256]{2,1,0:T(8,128)(2,1)}, bf16[3,128,256]{2,1,0:T(8,128)(2,1)S(1)}, u32[]{:S(2)}, u32[]{:S(2)}) collective-permute-start(bf16[3,128,256]{2,1,0:T(8,128)(2,1)} %get-tuple-element.50), channel_id=1, source_target_pairs={{0,8},{4,12},{8,0},{12,4},{1,9},{5,13},{9,1},{13,5},{2,10},{6,14},... | collective-permute-start | bytes 589832 | tf_op jit(solution)/shard_map/ppermute | solution.py:37
  151.1 61.8 %collective-permute-start.11 = (bf16[3,128,256]{2,1,0:T(8,128)(2,1)}, bf16[3,128,256]{2,1,0:T(8,128)(2,1)}, u32[]{:S(2)}, u32[]{:S(2)}) collective-permute-start(bf16[3,128,256]{2,1,0:T(8,128)(2,1)} %get-tuple-element.51), channel_id=1, source_target_pairs={{0,4},{4,0},{8,12},{12,8},{1,5},{5,1},{9,13},{13,9},{2,6},{6,2},{1... | collective-permute-start | bytes 589832 | tf_op jit(solution)/shard_map/ppermute | solution.py:37
  212.8 96.1 %collective-permute-start.20 = (bf16[9,256,256]{2,1,0:T(8,128)(2,1)}, bf16[9,256,256]{2,1,0:T(8,128)(2,1)S(1)}, u32[]{:S(2)}, u32[]{:S(2)}) collective-permute-start(bf16[9,256,256]{2,1,0:T(8,128)(2,1)} %get-tuple-element.61.refs_8_), channel_id=1, source_target_pairs={{0,16},{16,0},{1,17},{17,1},{2,18},{18,2},{3,19},{19,3},{4,20},{20... | collective-permute-start | bytes 3538952 | tf_op jit(solution)/shard_map/ppermute | solution.py:37
  226.6 4.6 collective-permute-start.13
  228.1 15.2 %collective-permute-start.6 = (bf16[3,256,256]{2,1,0:T(8,128)(2,1)}, bf16[3,256,256]{2,1,0:T(8,128)(2,1)S(1)}, u32[]{:S(2)}, u32[]{:S(2)}) collective-permute-start(bf16[3,256,256]{2,1,0:T(8,128)(2,1)} %hold.4.refs_0_), channel_id=1, source_target_pairs={{0,4},{4,0},{8,12},{12,8},{1,5},{5,1},{9,13},{13,9},{2,6},{6,2},{1... | collective-permute-start | bytes 1179656 | tf_op jit(solution)/shard_map/ppermute | solution.py:37
  229.1 14.2 %collective-permute-start.7 = (bf16[3,256,256]{2,1,0:T(8,128)(2,1)}, bf16[3,256,256]{2,1,0:T(8,128)(2,1)S(1)}, u32[]{:S(2)}, u32[]{:S(2)}) collective-permute-start(bf16[3,256,256]{2,1,0:T(8,128)(2,1)} %hold.4.refs_0_), channel_id=1, source_target_pairs={{0,8},{4,12},{8,0},{12,4},{1,9},{5,13},{9,1},{13,5},{2,10},{6,14},... | collective-permute-start | bytes 1179656 | tf_op jit(solution)/shard_map/ppermute | solution.py:37
  229.6 2.5 copy-start.23
  229.6 63.4 %collective-permute-start.18 = (bf16[3,128,256]{2,1,0:T(8,128)(2,1)}, bf16[3,128,256]{2,1,0:T(8,128)(2,1)S(1)}, u32[]{:S(2)}, u32[]{:S(2)}) collective-permute-start(bf16[3,128,256]{2,1,0:T(8,128)(2,1)} %get-tuple-element.62), channel_id=1, source_target_pairs={{0,8},{4,12},{8,0},{12,4},{1,9},{5,13},{9,1},{13,5},{2,10},{6,14},... | collective-permute-start | bytes 589832 | tf_op jit(solution)/shard_map/ppermute | solution.py:37
  231.2 61.9 %collective-permute-start.19 = (bf16[3,128,256]{2,1,0:T(8,128)(2,1)}, bf16[3,128,256]{2,1,0:T(8,128)(2,1)}, u32[]{:S(2)}, u32[]{:S(2)}) collective-permute-start(bf16[3,128,256]{2,1,0:T(8,128)(2,1)} %get-tuple-element.63), channel_id=1, source_target_pairs={{0,4},{4,0},{8,12},{12,8},{1,5},{5,1},{9,13},{13,9},{2,6},{6,2},{1... | collective-permute-start | bytes 589832 | tf_op jit(solution)/shard_map/ppermute | solution.py:37
  293.0 45.5 %collective-permute-start.22 = (bf16[9,256,256]{2,1,0:T(8,128)(2,1)}, bf16[9,256,256]{2,1,0:T(8,128)(2,1)}, u32[]{:S(2)}, u32[]{:S(2)}) collective-permute-start(bf16[9,256,256]{2,1,0:T(8,128)(2,1)} %get-tuple-element.58.refs_8_), channel_id=1, source_target_pairs={{0,16},{16,0},{1,17},{17,1},{2,18},{18,2},{3,19},{19,3},{4,20},{20... | collective-permute-start | bytes 3538952 | tf_op jit(solution)/shard_map/ppermute | solution.py:37
  306.8 2.1 collective-permute-start.21
  307.3 13.9 %collective-permute-start.14 = (bf16[3,128,256]{2,1,0:T(8,128)(2,1)}, bf16[3,128,256]{2,1,0:T(8,128)(2,1)S(1)}, u32[]{:S(2)}, u32[]{:S(2)}) collective-permute-start(bf16[3,128,256]{2,1,0:T(8,128)(2,1)} %get-tuple-element.59), channel_id=1, source_target_pairs={{0,8},{4,12},{8,0},{12,4},{1,9},{5,13},{9,1},{13,5},{2,10},{6,14},... | collective-permute-start | bytes 589832 | tf_op jit(solution)/shard_map/ppermute | solution.py:37
  307.8 13.4 %collective-permute-start.15 = (bf16[3,128,256]{2,1,0:T(8,128)(2,1)}, bf16[3,128,256]{2,1,0:T(8,128)(2,1)S(1)}, u32[]{:S(2)}, u32[]{:S(2)}) collective-permute-start(bf16[3,128,256]{2,1,0:T(8,128)(2,1)} %get-tuple-element.60), channel_id=1, source_target_pairs={{0,4},{4,0},{8,12},{12,8},{1,5},{5,1},{9,13},{13,9},{2,6},{6,2},{1... | collective-permute-start | bytes 589832 | tf_op jit(solution)/shard_map/ppermute | solution.py:37
  310.1 26.0 %copy-start.38 = (bf16[2048,64]{0,1:T(8,128)(2,1)S(1)}, bf16[2048,64]{0,1:T(8,128)(2,1)}, u32[]{:S(2)}) copy-start(bf16[2048,64]{0,1:T(8,128)(2,1)} %param.17) | copy-start | bytes 786436
  321.2 15.2 %copy-start.40 = (bf16[2048,64]{0,1:T(8,128)(2,1)S(1)}, bf16[2048,64]{0,1:T(8,128)(2,1)}, u32[]{:S(2)}) copy-start(bf16[2048,64]{0,1:T(8,128)(2,1)} %param.18) | copy-start | bytes 786436
  335.0 3.4 collective-permute-start.23
  355.4 5.6 %copy-start.18 = (bf16[512,512]{1,0:T(8,128)(2,1)S(1)}, bf16[512,512]{1,0:T(8,128)(2,1)}, u32[]{:S(2)}) copy-start(bf16[512,512]{1,0:T(8,128)(2,1)} %token_grad.9) | copy-start | bytes 1572868
  355.4 11.2 %copy-start.3 = (f32[1024,128]{1,0:T(8,128)S(1)}, f32[1024,128]{1,0:T(8,128)}, u32[]{:S(2)}) copy-start(f32[1024,128]{1,0:T(8,128)} %get-tuple-element.80.low_ref) | copy-start | bytes 1572868
  355.4 11.2 %copy-start.4 = (bf16[1024,2048]{1,0:T(8,128)(2,1)S(1)}, bf16[1024,2048]{1,0:T(8,128)(2,1)}, u32[]{:S(2)}) copy-start(bf16[1024,2048]{1,0:T(8,128)(2,1)} %refs_0_.7) | copy-start | bytes 12582916
  361.0 18.4 %collective-permute-start.24 = (bf16[512,512]{1,0:T(8,128)(2,1)S(1)}, bf16[512,512]{1,0:T(8,128)(2,1)}, u32[]{:S(2)}, u32[]{:S(2)}) collective-permute-start(bf16[512,512]{1,0:T(8,128)(2,1)S(1)} %copy-done.18), channel_id=1, source_target_pairs={{0,1},{3,2},{4,5},{7,6},{8,9},{11,10},{12,13},{15,14},{16,17},{19,... | collective-permute-start | bytes 1572872 | tf_op jit(solution)/shard_map/ppermute | solution.py:431
  365.3 22.8 %collective-permute-start.25 = (bf16[512,512]{1,0:T(8,128)(2,1)}, bf16[512,512]{1,0:T(8,128)(2,1)S(1)}, u32[]{:S(2)}, u32[]{:S(2)}) collective-permute-start(bf16[512,512]{1,0:T(8,128)(2,1)} %token_grad.11), channel_id=1, source_target_pairs={{0,1},{3,2},{4,5},{7,6},{8,9},{11,10},{12,13},{15,14},{16,17},{19,... | collective-permute-start | bytes 1572872 | tf_op jit(solution)/shard_map/ppermute | solution.py:431
  374.4 5.1 %copy-start.16 = (bf16[512,512]{1,0:T(8,128)(2,1)S(1)}, bf16[512,512]{1,0:T(8,128)(2,1)}, u32[]{:S(2)}) copy-start(bf16[512,512]{1,0:T(8,128)(2,1)} %token_grad.8) | copy-start | bytes 1572868
  380.6 9.4 %copy-start.15 = (bf16[512,512]{1,0:T(8,128)(2,1)}, bf16[512,512]{1,0:T(8,128)(2,1)S(1)}, u32[]{:S(2)}) copy-start(bf16[512,512]{1,0:T(8,128)(2,1)S(1)} %add_convert_fusion.7.refs_3_) | copy-start | bytes 1572868
  380.7 30.2 %collective-permute-start.26 = (bf16[512,512]{1,0:T(8,128)(2,1)S(1)}, bf16[512,512]{1,0:T(8,128)(2,1)S(1)}, u32[]{:S(2)}, u32[]{:S(2)}) collective-permute-start(bf16[512,512]{1,0:T(8,128)(2,1)S(1)} %add_convert_fusion.7.refs_3_), channel_id=1, source_target_pairs={{0,1},{1,2},{4,5},{5,6},{8,9},{9,10},{12,13},{13,14},{16,17},{17,1... | collective-permute-start | bytes 1572872 | tf_op jit(solution)/shard_map/ppermute | solution.py:431
  382.5 28.4 %collective-permute-start.28 = (bf16[512,512]{1,0:T(8,128)(2,1)S(1)}, bf16[512,512]{1,0:T(8,128)(2,1)S(1)}, u32[]{:S(2)}, u32[]{:S(2)}) collective-permute-start(bf16[512,512]{1,0:T(8,128)(2,1)S(1)} %add_convert_fusion.7.refs_3_), channel_id=1, source_target_pairs={{3,2},{2,1},{7,6},{6,5},{11,10},{10,9},{15,14},{14,13},{19,18},{18... | collective-permute-start | bytes 1572872 | tf_op jit(solution)/shard_map/ppermute | solution.py:431
  414.9 5.4 %copy-start.2 = (bf16[1024,1024]{1,0:T(8,128)(2,1)S(1)}, bf16[1024,1024]{1,0:T(8,128)(2,1)}, u32[]{:S(2)}) copy-start(bf16[1024,1024]{1,0:T(8,128)(2,1)} %get-tuple-element.85) | copy-start | bytes 6291460
  414.9 5.4 %copy-start.7 = (bf16[1024,64]{1,0:T(8,128)(2,1)S(1)}, bf16[1024,64]{1,0:T(8,128)(2,1)}, u32[]{:S(2)}) copy-start(bf16[1024,64]{1,0:T(8,128)(2,1)} %fusion.14.refs_2_) | copy-start | bytes 393220
  427.3 3.2 collective-permute-start.34
  427.3 12.0 %copy-start.13 = (bf16[512,512]{1,0:T(8,128)(2,1)S(1)}, bf16[512,512]{1,0:T(8,128)(2,1)}, u32[]{:S(2)}) copy-start(bf16[512,512]{1,0:T(8,128)(2,1)} %token_grad.13.refs_3_) | copy-start | bytes 1572868
  433.0 15.6 %copy-start.11 = (f32[4,384,192]{1,2,0:T(8,128)S(1)}, f32[4,384,192]{1,2,0:T(8,128)}, u32[]{:S(2)}) copy-start(f32[4,384,192]{1,2,0:T(8,128)} %copy-done.10) | copy-start | bytes 3538948
  433.0 15.5 %collective-permute-start.35 = (f32[2,384,192]{1,2,0:T(8,128)S(1)}, f32[2,384,192]{1,2,0:T(8,128)}, u32[]{:S(2)}, u32[]{:S(2)}) collective-permute-start(f32[2,384,192]{1,2,0:T(8,128)S(1)} %dynamic-slice_bitcast_fusion), channel_id=1, source_target_pairs={{0,8},{4,12},{8,0},{12,4},{1,9},{5,13},{9,1},{13,5},{2,10},{6,14},... | collective-permute-start | bytes 1769480 | tf_op jit(solution)/shard_map/ppermute | solution.py:37
  434.2 17.0 %copy-start.12 = (bf16[512,512]{1,0:T(8,128)(2,1)S(1)}, bf16[512,512]{1,0:T(8,128)(2,1)}, u32[]{:S(2)}) copy-start(bf16[512,512]{1,0:T(8,128)(2,1)} %token_grad.15.refs_4_) | copy-start | bytes 1572868
  434.2 17.0 %copy-start.17 = (bf16[512,512]{1,0:T(8,128)(2,1)S(1)}, bf16[512,512]{1,0:T(8,128)(2,1)}, u32[]{:S(2)}) copy-start(bf16[512,512]{1,0:T(8,128)(2,1)} %token_grad.11) | copy-start | bytes 1572868
  434.2 17.0 %collective-permute-start.30 = (bf16[512,512]{1,0:T(8,128)(2,1)}, bf16[512,512]{1,0:T(8,128)(2,1)S(1)}, u32[]{:S(2)}, u32[]{:S(2)}) collective-permute-start(bf16[512,512]{1,0:T(8,128)(2,1)} %add_convert_fusion.6.refs_4_), channel_id=1, source_target_pairs={{0,1},{1,2},{4,5},{5,6},{8,9},{9,10},{12,13},{13,14},{16,17},{17,1... | collective-permute-start | bytes 1572872 | tf_op jit(solution)/shard_map/ppermute | solution.py:431
  438.6 12.6 %collective-permute-start.32 = (bf16[512,512]{1,0:T(8,128)(2,1)}, bf16[512,512]{1,0:T(8,128)(2,1)S(1)}, u32[]{:S(2)}, u32[]{:S(2)}) collective-permute-start(bf16[512,512]{1,0:T(8,128)(2,1)} %add_convert_fusion.6.refs_4_), channel_id=1, source_target_pairs={{3,2},{2,1},{7,6},{6,5},{11,10},{10,9},{15,14},{14,13},{19,18},{18... | collective-permute-start | bytes 1572872 | tf_op jit(solution)/shard_map/ppermute | solution.py:431
  441.0 21.3 %collective-permute-start.27 = (bf16[512,512]{1,0:T(8,128)(2,1)S(1)}, bf16[512,512]{1,0:T(8,128)(2,1)S(1)}, u32[]{:S(2)}, u32[]{:S(2)}) collective-permute-start(bf16[512,512]{1,0:T(8,128)(2,1)S(1)} %get-tuple-element.87), channel_id=1, source_target_pairs={{0,1},{1,2},{2,3},{4,5},{5,6},{6,7},{8,9},{9,10},{10,11},{12,13},{... | collective-permute-start | bytes 1572872 | tf_op jit(solution)/shard_map/ppermute | solution.py:431
  445.1 17.3 %collective-permute-start.29 = (bf16[512,512]{1,0:T(8,128)(2,1)S(1)}, bf16[512,512]{1,0:T(8,128)(2,1)S(1)}, u32[]{:S(2)}, u32[]{:S(2)}) collective-permute-start(bf16[512,512]{1,0:T(8,128)(2,1)S(1)} %get-tuple-element.88), channel_id=1, source_target_pairs={{3,2},{2,1},{1,0},{7,6},{6,5},{5,4},{11,10},{10,9},{9,8},{15,14},{... | collective-permute-start | bytes 1572872 | tf_op jit(solution)/shard_map/ppermute | solution.py:431
  449.6 12.7 %copy-start.6 = (f32[512,512]{1,0:T(8,128)S(1)}, f32[512,512]{1,0:T(8,128)}, u32[]{:S(2)}) copy-start(f32[512,512]{1,0:T(8,128)} %token_grad.12.refs_5_) | copy-start | bytes 3145732
  449.7 12.9 %collective-permute-start.36 = (f32[1,384,192]{1,2,0:T(8,128)S(1)}, f32[1,384,192]{1,2,0:T(8,128)S(1)}, u32[]{:S(2)}, u32[]{:S(2)}) collective-permute-start(f32[1,384,192]{1,2,0:T(8,128)S(1)} %constant_dynamic-slice_fusion.2), channel_id=1, source_target_pairs={{0,4},{4,0},{8,12},{12,8},{1,5},{5,1},{9,13},{13,9},{2,6},{6,2},{1... | collective-permute-start | bytes 884744 | tf_op jit(solution)/shard_map/ppermute | solution.py:37
  452.5 21.1 %collective-permute-start.31 = (bf16[512,512]{1,0:T(8,128)(2,1)}, bf16[512,512]{1,0:T(8,128)(2,1)S(1)}, u32[]{:S(2)}, u32[]{:S(2)}) collective-permute-start(bf16[512,512]{1,0:T(8,128)(2,1)} %get-tuple-element.89), channel_id=1, source_target_pairs={{0,1},{1,2},{2,3},{4,5},{5,6},{6,7},{8,9},{9,10},{10,11},{12,13},{... | collective-permute-start | bytes 1572872 | tf_op jit(solution)/shard_map/ppermute | solution.py:431
  460.4 13.3 %copy-start.5 = (f32[512,512]{1,0:T(8,128)S(1)}, f32[512,512]{1,0:T(8,128)}, u32[]{:S(2)}) copy-start(f32[512,512]{1,0:T(8,128)} %token_grad.14.refs_6_) | copy-start | bytes 3145732
  460.4 13.2 %collective-permute-start.33 = (bf16[512,512]{1,0:T(8,128)(2,1)}, bf16[512,512]{1,0:T(8,128)(2,1)}, u32[]{:S(2)}, u32[]{:S(2)}) collective-permute-start(bf16[512,512]{1,0:T(8,128)(2,1)} %get-tuple-element.90), channel_id=1, source_target_pairs={{3,2},{2,1},{1,0},{7,6},{6,5},{5,4},{11,10},{10,9},{9,8},{15,14},{... | collective-permute-start | bytes 1572872 | tf_op jit(solution)/shard_map/ppermute | solution.py:431
  462.7 6.4 %collective-permute-start.39 = (f32[128,192]{0,1:T(8,128)S(1)}, f32[128,192]{0,1:T(8,128)S(1)}, u32[]{:S(2)}, u32[]{:S(2)}) collective-permute-start(f32[128,192]{0,1:T(8,128)S(1)} %slice_bitcast_fusion.8), channel_id=1, source_target_pairs={{0,4},{4,0},{8,12},{12,8},{1,5},{5,1},{9,13},{13,9},{2,6},{6,2},{1... | collective-permute-start | bytes 294920 | tf_op jit(solution)/shard_map/ppermute | solution.py:37
  464.0 17.8 %collective-permute-start.37 = (f32[128,192]{0,1:T(8,128)S(1)}, f32[128,192]{0,1:T(8,128)S(1)}, u32[]{:S(2)}, u32[]{:S(2)}) collective-permute-start(f32[128,192]{0,1:T(8,128)S(1)} %bitcast.94), channel_id=1, source_target_pairs={{0,2},{1,3},{2,0},{3,1},{4,6},{5,7},{6,4},{7,5},{8,10},{9,11},{10,... | collective-permute-start | bytes 294920 | tf_op jit(solution)/shard_map/ppermute | solution.py:37
  469.1 12.9 %collective-permute-start.40 = (f32[256,192]{0,1:T(8,128)S(1)}, f32[256,192]{0,1:T(8,128)S(1)}, u32[]{:S(2)}, u32[]{:S(2)}) collective-permute-start(f32[256,192]{0,1:T(8,128)S(1)} %maximum_select_fusion.2), channel_id=1, source_target_pairs={{0,8},{4,12},{8,0},{12,4},{1,9},{5,13},{9,1},{13,5},{2,10},{6,14},... | collective-permute-start | bytes 589832 | tf_op jit(solution)/shard_map/ppermute | solution.py:37
  481.9 6.3 %copy-start.1 = (bf16[2048,64]{0,1:T(8,128)(2,1)S(1)}, bf16[2048,64]{0,1:T(8,128)(2,1)}, u32[]{:S(2)}) copy-start(bf16[2048,64]{0,1:T(8,128)(2,1)} %param.22) | copy-start | bytes 786436
  482.0 5.2 %collective-permute-start.41 = (f32[512,192]{0,1:T(8,128)S(1)}, f32[512,192]{0,1:T(8,128)S(1)}, u32[]{:S(2)}, u32[]{:S(2)}) collective-permute-start(f32[512,192]{0,1:T(8,128)S(1)} %maximum_select_fusion.1), channel_id=1, source_target_pairs={{0,16},{16,0},{1,17},{17,1},{2,18},{18,2},{3,19},{19,3},{4,20},{20... | collective-permute-start | bytes 1179656 | tf_op jit(solution)/shard_map/ppermute | solution.py:37
  482.1 4.5 collective-permute-start.38
  (23 other events, 22.1 us)
